TPU v7x, 32 devices: a whole 2x2x4 slice. The times are simulated.
32 devices in a mesh: dp: 16 (over z, y, x), rep: 2 (over core).
Axes of the slice: x: 2, y: 2, z: 4, core: 2. Of those that a mesh axis runs over, the one named last changes fastest.
Arguments:
- images: bfloat16 [2, 512, 16, 512], P(None, ('dp', 'rep')), may hold values from -6 to 6
- lengths: int32 [2, 7], replicated, may hold values from 1 to 128, 256 in all within a row
- widths: int32 [2, 7], replicated, may hold values from 8 to 16
- conv_one: bfloat16 [3, 3, 512, 512], P(None, None, 'dp'), may hold values from -0.09375 to 0.09375
- conv_two: bfloat16 [3, 3, 512, 512], P(None, None, 'dp'), may hold values from -0.09375 to 0.09375
- squeeze: bfloat16 [3, 512, 128], P(None, 'dp'), may hold values from -0.25 to 0.25
- expand: bfloat16 [3, 128, 512], P(None, 'dp'), may hold values from -0.5 to 0.5
- task_conv: bfloat16 [3, 3, 3, 512, 512], P(None, None, None, 'dp'), may hold values from -0.09375 to 0.09375
- gains_shared: float32 [2, 512], replicated, may hold values from 0.25 to 1.75
- biases_shared: float32 [2, 512], replicated, may hold values from -2.5 to 2.5
- gains_squeeze: float32 [3, 128], replicated, may hold values from 0.25 to 1.75
- biases_squeeze: float32 [3, 128], replicated, may hold values from -2.5 to 2.5
- gains_expand: float32 [3, 512], replicated, may hold values from 0.25 to 1.75
- biases_expand: float32 [3, 512], replicated, may hold values from -2.5 to 2.5
- gains_task: float32 [3, 512], replicated, may hold values from 0.25 to 1.75
- biases_task: float32 [3, 512], replicated, may hold values from -2.5 to 2.5
- loss_history: float32 [3, 2], replicated, may hold values from 0.5 to 2
- cotangent: bfloat16 [3, 2, 256, 8, 512], P(None, None, ('dp', 'rep')), may hold values from -6 to 6
Outputs:
- features: float32 [3, 2, 256, 8, 512], P(None, None, ('dp', 'rep'))
- input_grad: float32 [2, 512, 16, 512], P(None, ('dp', 'rep'))
- grad_conv_one: float32 [3, 3, 512, 512], P(None, None, 'dp')
- grad_conv_two: float32 [3, 3, 512, 512], P(None, None, 'dp')
- grad_squeeze: float32 [3, 512, 128], P(None, 'dp')
- grad_expand: float32 [3, 128, 512], P(None, 'dp')
- grad_task_conv: float32 [3, 3, 3, 512, 512], P(None, None, None, 'dp')
- grad_gains_shared: float32 [2, 512], replicated
- grad_biases_shared: float32 [2, 512], replicated
- grad_gains_squeeze: float32 [3, 128], replicated
- grad_biases_squeeze: float32 [3, 128], replicated
- grad_gains_expand: float32 [3, 512], replicated
- grad_biases_expand: float32 [3, 512], replicated
- grad_gains_task: float32 [3, 512], replicated
- grad_biases_task: float32 [3, 512], replicated
Inputs may be any that keep to these rules, and one draw needn't show every extreme that they name: `lengths`: the 7 entries of a micro-batch sum to 256 and the largest equals 128; an image's height is twice its entry. `widths`: columns from an image's width on are padding.
All inputs are finite; a program needn't handle non-finite values.
Results may differ from a plain program's by a relative error of at most 0.015.
Values may be sent and summed in bfloat16 or wider, within the bound.
No kernel may reach another device: no remote copies, remote signals or barrier semaphores. Data moves between devices by JAX's collectives and lax.ppermute only.
A program may use at most 256 MiB of HBM per device.

v0:
```python
import jax
import jax.numpy as jnp
from jax import lax
from jax.sharding import PartitionSpec as P

EPSILON = 1e-05


def with_halo(block, sides, width):
    for axis, dim in sides:
        count = lax.axis_size(axis)
        forward = [(i, i + 1) for i in range(count - 1)]
        backward = [(target, source) for source, target in forward]
        low = lax.ppermute(
            lax.slice_in_dim(block, block.shape[dim] - width, None, axis=dim), axis, forward
        )
        high = lax.ppermute(lax.slice_in_dim(block, 0, width, axis=dim), axis, backward)
        block = jnp.concatenate([low, block, high], axis=dim)
    return block


def layout(length_row, width_row, offset, row_count, col_count):
    image_count = length_row.shape[0]
    image_ends = 2 * jnp.cumsum(length_row)
    starts = image_ends - 2 * length_row
    places = offset + jnp.arange(row_count + 1, dtype=jnp.int32)
    image_index = jnp.sum((places[:, None] >= image_ends[None, :]).astype(jnp.int32), axis=1)
    member = (image_index[:, None] == jnp.arange(image_count, dtype=jnp.int32)[None, :]).astype(
        jnp.int32
    )
    first_row = jnp.sum((places[:, None] == starts[None, :]).astype(jnp.float32), axis=1)
    linked = 1.0 - first_row
    row_width = jnp.sum(member * width_row[None, :], axis=1)
    columns = jnp.arange(col_count, dtype=jnp.int32)
    pixel_mask = (columns[None, :] < row_width[:row_count, None]).astype(jnp.float32)
    return (pixel_mask, linked[:row_count], linked[1:])


def silu_slope(values):
    logistic = jax.nn.sigmoid(values)
    return logistic * (1.0 + values * (1.0 - logistic))


def rows_forward(activation):
    return with_halo(activation, ((("dp", "rep"), 1),), 1)


def unfold(padded, up_flag, down_flag):
    row_count = padded.shape[1] - 2
    col_count = padded.shape[2]
    framed = jnp.pad(padded, ((0, 0), (0, 0), (1, 1), (0, 0)))
    factors = (up_flag, jnp.ones_like(up_flag), down_flag)
    pieces = []
    for tap_row in range(3):
        row_scale = factors[tap_row].astype(padded.dtype)[None, :, None, None]
        for tap_col in range(3):
            pieces.append(
                framed[:, tap_row : tap_row + row_count, tap_col : tap_col + col_count] * row_scale
            )
    return jnp.stack(pieces, axis=1)


def conv_back(grad_low, weight_nine, up_flag, down_flag):
    padded = with_halo(grad_low, ((("dp", "rep"), 1),), 1)
    row_count = grad_low.shape[1]
    col_count = grad_low.shape[2]
    framed = jnp.pad(padded, ((0, 0), (0, 0), (1, 1), (0, 0)))
    factors = (down_flag, jnp.ones_like(down_flag), up_flag)
    pieces = []
    for tap_row in range(3):
        row_scale = factors[tap_row].astype(grad_low.dtype)[None, :, None, None]
        for tap_col in range(3):
            top = 2 - tap_row
            left = 2 - tap_col
            pieces.append(framed[:, top : top + row_count, left : left + col_count] * row_scale)
    return jnp.einsum(
        "knrwd,kncd->krwc",
        jnp.stack(pieces, axis=1),
        weight_nine,
        preferred_element_type=jnp.float32,
    )


def normalize(values, valid_mask):
    local_count = jnp.sum(valid_mask)
    masked = values * valid_mask
    first_sum, pixel_count = lax.psum((jnp.sum(masked, axis=(1, 2)), local_count), ("dp", "rep"))
    mean_value = first_sum / pixel_count
    centered = (values - mean_value[:, None, None, :]) * valid_mask
    spread = lax.psum(jnp.sum(centered * centered, axis=(1, 2)), ("dp", "rep"))
    variance = spread / pixel_count
    inverse = lax.rsqrt(variance + EPSILON)
    scaled = (values - mean_value[:, None, None, :]) * inverse[:, None, None, :]
    return (scaled, inverse, pixel_count)


def normalize_back(grad_out, scaled, inverse, pixel_count, gain_row, valid_mask):
    shift_grad, gain_grad = lax.psum(
        (
            jnp.sum(grad_out * valid_mask, axis=(1, 2)),
            jnp.sum(grad_out * scaled * valid_mask, axis=(1, 2)),
        ),
        ("dp", "rep"),
    )
    factor = (gain_row * inverse)[:, None, None, :]
    grad_in = (
        valid_mask
        * factor
        * (
            grad_out
            - (shift_grad / pixel_count)[:, None, None, :]
            - scaled * (gain_grad / pixel_count)[:, None, None, :]
        )
    )
    return (grad_in.astype(jnp.bfloat16), gain_grad, shift_grad)


def add_tuple(left_items, right_items):
    if left_items is None:
        return right_items
    return tuple((left_part + right_part for left_part, right_part in zip(left_items, right_items)))


def local(
    images,
    lengths,
    widths,
    conv_one,
    conv_two,
    squeeze,
    expand,
    task_conv,
    gains_shared,
    biases_shared,
    gains_squeeze,
    biases_squeeze,
    gains_expand,
    biases_expand,
    gains_task,
    biases_task,
    loss_history,
    cotangent,
):
    batch_count, row_count, col_count, channel_count = images.shape
    task_count = cotangent.shape[0]
    offset = lax.axis_index(("dp", "rep")) * row_count
    loss_ratio = loss_history[:, 1] / loss_history[:, 0]
    task_scale = task_count * jax.nn.softmax(loss_ratio / 2.0)
    feature_list = []
    input_list = []
    weight_sums = None
    norm_sums = None
    for batch_index in range(batch_count):
        full_one, full_two, full_squeeze, full_expand, full_task = (
            lax.all_gather(conv_one, "dp", axis=2, tiled=True),
            lax.all_gather(conv_two, "dp", axis=2, tiled=True),
            lax.all_gather(squeeze, "dp", axis=1, tiled=True),
            lax.all_gather(expand, "dp", axis=1, tiled=True),
            lax.all_gather(task_conv, "dp", axis=3, tiled=True),
        )
        nine_one = full_one.reshape(1, 9, channel_count, channel_count)
        nine_two = full_two.reshape(1, 9, channel_count, channel_count)
        nine_task = full_task.reshape(task_count, 9, channel_count, channel_count)
        pixel_mask, up_flag, down_flag = layout(
            lengths[batch_index], widths[batch_index], offset, row_count, col_count
        )
        valid_mask = pixel_mask[None, :, :, None]
        entering = images[batch_index][None] * valid_mask.astype(jnp.bfloat16)
        unfolded_one = unfold(rows_forward(entering), up_flag, down_flag)
        conv_first = jnp.einsum(
            "knrwc,kncd->krwd", unfolded_one, nine_one, preferred_element_type=jnp.float32
        )
        scaled_one, inverse_one, pixel_count = normalize(conv_first, valid_mask)
        level_one = (
            gains_shared[0:1][:, None, None, :] * scaled_one + biases_shared[0:1][:, None, None, :]
        )
        hidden_one = (valid_mask * jax.nn.silu(level_one)).astype(jnp.bfloat16)
        unfolded_two = unfold(rows_forward(hidden_one), up_flag, down_flag)
        conv_second = jnp.einsum(
            "knrwc,kncd->krwd", unfolded_two, nine_two, preferred_element_type=jnp.float32
        )
        scaled_two, inverse_two, pixel_count = normalize(conv_second, valid_mask)
        level_two = (
            gains_shared[1:2][:, None, None, :] * scaled_two + biases_shared[1:2][:, None, None, :]
        )
        shared = valid_mask * jax.nn.silu(level_two)
        shared_low = shared.astype(jnp.bfloat16)
        squeezed = jnp.einsum(
            "rwc,tcb->trwb", shared_low[0], full_squeeze, preferred_element_type=jnp.float32
        )
        scaled_narrow, inverse_narrow, pixel_count = normalize(squeezed, valid_mask)
        level_narrow = (
            gains_squeeze[:, None, None, :] * scaled_narrow + biases_squeeze[:, None, None, :]
        )
        narrow = (valid_mask * jax.nn.silu(level_narrow)).astype(jnp.bfloat16)
        expanded = jnp.einsum(
            "trwb,tbc->trwc", narrow, full_expand, preferred_element_type=jnp.float32
        )
        scaled_wide, inverse_wide, pixel_count = normalize(expanded, valid_mask)
        level_wide = gains_expand[:, None, None, :] * scaled_wide + biases_expand[:, None, None, :]
        logistic_wide = jax.nn.sigmoid(level_wide)
        attention = valid_mask * logistic_wide
        gated_low = (attention * shared).astype(jnp.bfloat16)
        unfolded_task = unfold(rows_forward(gated_low), up_flag, down_flag)
        task_out = jnp.einsum(
            "knrwc,kncd->krwd", unfolded_task, nine_task, preferred_element_type=jnp.float32
        )
        scaled_task, inverse_task, pixel_count = normalize(task_out, valid_mask)
        level_task = gains_task[:, None, None, :] * scaled_task + biases_task[:, None, None, :]
        finished = valid_mask * jax.nn.silu(level_task)
        shaped = finished.reshape(task_count, row_count // 2, 2, col_count // 2, 2, channel_count)
        feature_list.append(0.25 * jnp.sum(shaped, axis=(2, 4)))
        upstream = task_scale[:, None, None, None] * cotangent[:, batch_index].astype(jnp.float32)
        spread_grad = 0.25 * jnp.broadcast_to(
            upstream[:, :, None, :, None, :],
            (task_count, row_count // 2, 2, col_count // 2, 2, channel_count),
        ).reshape(task_count, row_count, col_count, channel_count)
        grad_level = spread_grad * valid_mask * silu_slope(level_task)
        task_low, gain_task_part, shift_task_part = normalize_back(
            grad_level, scaled_task, inverse_task, pixel_count, gains_task, valid_mask
        )
        weight_grad_task = jnp.einsum(
            "knrwc,krwd->kncd", unfolded_task, task_low, preferred_element_type=jnp.float32
        ).reshape(task_count, 3, 3, channel_count, channel_count)
        grad_gated = conv_back(task_low, nine_task, up_flag, down_flag)
        grad_wide_level = grad_gated * shared * valid_mask * logistic_wide * (1.0 - logistic_wide)
        wide_low, gain_wide_part, shift_wide_part = normalize_back(
            grad_wide_level, scaled_wide, inverse_wide, pixel_count, gains_expand, valid_mask
        )
        weight_grad_expand = jnp.einsum(
            "trwb,trwc->tbc", narrow, wide_low, preferred_element_type=jnp.float32
        )
        grad_narrow = jnp.einsum(
            "trwc,tbc->trwb", wide_low, full_expand, preferred_element_type=jnp.float32
        )
        grad_narrow_level = grad_narrow * valid_mask * silu_slope(level_narrow)
        narrow_low, gain_narrow_part, shift_narrow_part = normalize_back(
            grad_narrow_level, scaled_narrow, inverse_narrow, pixel_count, gains_squeeze, valid_mask
        )
        weight_grad_squeeze = jnp.einsum(
            "rwc,trwb->tcb", shared_low[0], narrow_low, preferred_element_type=jnp.float32
        )
        grad_shared = jnp.einsum(
            "trwb,tcb->rwc", narrow_low, full_squeeze, preferred_element_type=jnp.float32
        ) + jnp.sum(grad_gated * attention, axis=0)
        grad_level_two = grad_shared[None] * valid_mask * silu_slope(level_two)
        second_low, gain_two_part, shift_two_part = normalize_back(
            grad_level_two, scaled_two, inverse_two, pixel_count, gains_shared[1:2], valid_mask
        )
        weight_grad_two = jnp.einsum(
            "knrwc,krwd->kncd", unfolded_two, second_low, preferred_element_type=jnp.float32
        ).reshape(3, 3, channel_count, channel_count)
        grad_hidden = conv_back(second_low, nine_two, up_flag, down_flag)
        grad_level_one = grad_hidden * valid_mask * silu_slope(level_one)
        first_low, gain_one_part, shift_one_part = normalize_back(
            grad_level_one, scaled_one, inverse_one, pixel_count, gains_shared[0:1], valid_mask
        )
        weight_grad_one = jnp.einsum(
            "knrwc,krwd->kncd", unfolded_one, first_low, preferred_element_type=jnp.float32
        ).reshape(3, 3, channel_count, channel_count)
        grad_entering = conv_back(first_low, nine_one, up_flag, down_flag)
        input_list.append((valid_mask * grad_entering)[0])
        norm_sums = add_tuple(
            norm_sums,
            (
                jnp.concatenate([gain_one_part, gain_two_part], axis=0),
                jnp.concatenate([shift_one_part, shift_two_part], axis=0),
                gain_narrow_part,
                shift_narrow_part,
                gain_wide_part,
                shift_wide_part,
                gain_task_part,
                shift_task_part,
            ),
        )
        shard_part = (
            lax.psum_scatter(weight_grad_one, "dp", scatter_dimension=2, tiled=True),
            lax.psum_scatter(weight_grad_two, "dp", scatter_dimension=2, tiled=True),
            lax.psum_scatter(weight_grad_squeeze, "dp", scatter_dimension=1, tiled=True),
            lax.psum_scatter(weight_grad_expand, "dp", scatter_dimension=1, tiled=True),
            lax.psum_scatter(weight_grad_task, "dp", scatter_dimension=3, tiled=True),
        )
        weight_sums = add_tuple(weight_sums, shard_part)
    summed = (
        lax.psum(weight_sums[0].astype(jnp.bfloat16), "rep").astype(jnp.float32),
        lax.psum(weight_sums[1].astype(jnp.bfloat16), "rep").astype(jnp.float32),
        lax.psum(weight_sums[2].astype(jnp.bfloat16), "rep").astype(jnp.float32),
        lax.psum(weight_sums[3].astype(jnp.bfloat16), "rep").astype(jnp.float32),
        lax.psum(weight_sums[4].astype(jnp.bfloat16), "rep").astype(jnp.float32),
    )
    features = jnp.stack(feature_list, axis=1)
    input_grad = jnp.stack(input_list, axis=0)
    return (
        features,
        input_grad,
        summed[0],
        summed[1],
        summed[2],
        summed[3],
        summed[4],
        norm_sums[0],
        norm_sums[1],
        norm_sums[2],
        norm_sums[3],
        norm_sums[4],
        norm_sums[5],
        norm_sums[6],
        norm_sums[7],
    )


def solution(mesh):
    placed = (
        P(None, ("dp", "rep"), None, None),
        P(),
        P(),
        P(None, None, "dp", None),
        P(None, None, "dp", None),
        P(None, "dp", None),
        P(None, "dp", None),
        P(None, None, None, "dp", None),
        P(),
        P(),
        P(),
        P(),
        P(),
        P(),
        P(),
        P(),
        P(),
        P(None, None, ("dp", "rep"), None, None),
    )
    return jax.shard_map(
        local,
        mesh=mesh,
        in_specs=placed,
        out_specs=(
            P(None, None, ("dp", "rep"), None, None),
            P(None, ("dp", "rep"), None, None),
            P(None, None, "dp", None),
            P(None, None, "dp", None),
            P(None, "dp", None),
            P(None, "dp", None),
            P(None, None, None, "dp", None),
            P(),
            P(),
            P(),
            P(),
            P(),
            P(),
            P(),
            P(),
        ),
        check_vma=False,
    )
```

profile of v0, /device:TPU:0, one launch (start us, length us, event | category | flops | bytes accessed | tf_op | source)
XLA Modules:
  0.0 2079.0 jit_solution(15293911787017776772)
XLA Ops:
  12.2 2.4 collective-permute-start.6
  15.9 5.1 collective-permute-start
  25.0 47.7 %all_gather.22 = bf16[3,512,128]{2,1,0:T(8,128)(2,1)S(1)} all-gather(bf16[3,32,128]{2,1,0:T(8,128)(2,1)S(1)} %copy-done.111), channel_id=1, replica_groups=mesh['dp'=16,'rep'=2] {'dp'}, dimensions={1}, use_global_device_ids=true | all-gather | bytes 417792 | tf_op jit(solution)/shard_map/all_gather | solution.py:157
  72.7 39.9 %all_gather.23 = bf16[3,128,512]{2,1,0:T(8,128)(2,1)S(1)} all-gather(bf16[3,8,512]{2,1,0:T(8,128)(2,1)S(1)} %copy-done.112), channel_id=1, replica_groups=mesh['dp'=16,'rep'=2] {'dp'}, dimensions={1}, use_global_device_ids=true | all-gather | bytes 417792 | tf_op jit(solution)/shard_map/all_gather | solution.py:158
  117.0 2.2 reshape.643
  120.0 2.3 reshape.646
  132.3 4.6 multiply_reduce_fusion.29
  136.9 3.3 multiply_reduce_fusion.33
  140.2 39.6 %all-reduce.27 = (f32[1,512]{1,0:T(1,128)S(1)}, f32[]{:T(128)}, f32[1,512]{1,0:T(1,128)S(1)}, f32[]{:T(128)}) all-reduce(f32[1,512]{1,0:T(1,128)S(1)} %bitcast.949, f32[]{:T(128)} %convert_reduce_fusion.1, f32[1,512]{1,0:T(1,128)S(1)} %bitcast.948, f32[]{:T(128)} %convert_reduce_fusion), channel_id=1, replica_groups=mesh['dp'=16,'rep'=2] {'dp','rep'}, use_global_device_ids=true, to_apply=%region_5.6 | all-reduce | flops 1026 | bytes 8208 | tf_op jit(solution)/shard_map/psum | solution.py:87
  181.3 43.5 %all-reduce.26 = (f32[1,512]{1,0:T(1,128)S(1)}, f32[1,512]{1,0:T(1,128)S(1)}) all-reduce(f32[1,512]{1,0:T(1,128)S(1)} %bitcast.929, f32[1,512]{1,0:T(1,128)S(1)} %bitcast.931), channel_id=1, replica_groups=mesh['dp'=16,'rep'=2] {'dp','rep'}, use_global_device_ids=true, to_apply=%region_9.10 | all-reduce | flops 1024 | bytes 8192 | tf_op jit(solution)/shard_map/psum | solution.py:90
  229.8 5.5 collective-permute-start.2
  237.1 2.6 collective-permute-done.3
  249.3 4.7 multiply_reduce_fusion.31
  254.1 3.3 multiply_reduce_fusion.27
  257.3 45.6 %all-reduce.25 = (f32[1,512]{1,0:T(1,128)S(1)}, f32[1,512]{1,0:T(1,128)S(1)}) all-reduce(f32[1,512]{1,0:T(1,128)S(1)} %bitcast.950, f32[1,512]{1,0:T(1,128)S(1)} %bitcast.951), channel_id=1, replica_groups=mesh['dp'=16,'rep'=2] {'dp','rep'}, use_global_device_ids=true, to_apply=%region_11.12 | all-reduce | flops 1024 | bytes 8192 | tf_op jit(solution)/shard_map/psum | solution.py:87
  304.4 44.3 %all-reduce.24 = (f32[1,512]{1,0:T(1,128)S(1)}, f32[1,512]{1,0:T(1,128)S(1)}) all-reduce(f32[1,512]{1,0:T(1,128)S(1)} %bitcast.930, f32[1,512]{1,0:T(1,128)S(1)} %bitcast.932), channel_id=1, replica_groups=mesh['dp'=16,'rep'=2] {'dp','rep'}, use_global_device_ids=true, to_apply=%region_13.14 | all-reduce | flops 1024 | bytes 8192 | tf_op jit(solution)/shard_map/psum | solution.py:90
  352.6 42.0 %all-reduce.23 = (f32[3,128]{1,0:T(4,128)S(1)}, f32[3,128]{1,0:T(4,128)S(1)}) all-reduce(f32[3,128]{1,0:T(4,128)S(1)} %get-tuple-element.259, f32[3,128]{1,0:T(4,128)S(1)} %get-tuple-element.261), channel_id=1, replica_groups=mesh['dp'=16,'rep'=2] {'dp','rep'}, use_global_device_ids=true, to_apply=%region_15.16 | all-reduce | flops 768 | bytes 6144 | tf_op jit(solution)/shard_map/psum | solution.py:87
  396.1 38.2 %all-reduce.22 = (f32[3,128]{1,0:T(4,128)S(1)}, f32[3,128]{1,0:T(4,128)S(1)}) all-reduce(f32[3,128]{1,0:T(4,128)S(1)} %multiply_reduce_fusion.38, f32[3,128]{1,0:T(4,128)S(1)} %multiply_reduce_fusion.36), channel_id=1, replica_groups=mesh['dp'=16,'rep'=2] {'dp','rep'}, use_global_device_ids=true, to_apply=%region_17.18 | all-reduce | flops 768 | bytes 6144 | tf_op jit(solution)/shard_map/psum | solution.py:90
  438.7 42.3 %all-reduce.21 = (f32[3,512]{1,0:T(4,128)S(1)}, f32[3,512]{1,0:T(4,128)S(1)}) all-reduce(f32[3,512]{1,0:T(4,128)} %get-tuple-element.263, f32[3,512]{1,0:T(4,128)} %get-tuple-element.265), channel_id=1, replica_groups=mesh['dp'=16,'rep'=2] {'dp','rep'}, use_global_device_ids=true, to_apply=%region_19.20 | all-reduce | flops 3072 | bytes 24576 | tf_op jit(solution)/shard_map/psum | solution.py:87
  482.8 38.9 %all-reduce.20 = (f32[3,512]{1,0:T(4,128)S(1)}, f32[3,512]{1,0:T(4,128)S(1)}) all-reduce(f32[3,512]{1,0:T(4,128)S(1)} %multiply_reduce_fusion.16, f32[3,512]{1,0:T(4,128)S(1)} %multiply_reduce_fusion.12), channel_id=1, replica_groups=mesh['dp'=16,'rep'=2] {'dp','rep'}, use_global_device_ids=true, to_apply=%region_21.22 | all-reduce | flops 3072 | bytes 24576 | tf_op jit(solution)/shard_map/psum | solution.py:90
  523.5 2.3 multiply_convert_fusion.4
  528.5 5.5 collective-permute-start.10
  536.1 2.4 collective-permute-done.11
  550.6 2.9 copy-done.83
  554.8 6.7 copy.109
  561.4 10.2 fusion.32
  571.9 9.1 fusion.29
  581.2 44.2 %all-reduce.19 = (f32[3,512]{1,0:T(4,128)S(1)}, f32[3,512]{1,0:T(4,128)S(1)}) all-reduce(f32[3,512]{1,0:T(4,128)S(1)} %multiply_reduce_fusion.15, f32[3,512]{1,0:T(4,128)S(1)} %multiply_reduce_fusion.11), channel_id=1, replica_groups=mesh['dp'=16,'rep'=2] {'dp','rep'}, use_global_device_ids=true, to_apply=%region_23.24 | all-reduce | flops 3072 | bytes 24576 | tf_op jit(solution)/shard_map/psum | solution.py:87
  627.3 41.2 %all-reduce.18 = (f32[3,512]{1,0:T(4,128)S(1)}, f32[3,512]{1,0:T(4,128)S(1)}) all-reduce(f32[3,512]{1,0:T(4,128)S(1)} %multiply_reduce_fusion.14, f32[3,512]{1,0:T(4,128)S(1)} %multiply_reduce_fusion.10), channel_id=1, replica_groups=mesh['dp'=16,'rep'=2] {'dp','rep'}, use_global_device_ids=true, to_apply=%region_25.26 | all-reduce | flops 3072 | bytes 24576 | tf_op jit(solution)/shard_map/psum | solution.py:90
  669.7 5.5 multiply_reduce_fusion.9
  675.2 39.5 %all-reduce.17 = (f32[3,512]{1,0:T(4,128)S(1)}, f32[3,512]{1,0:T(4,128)S(1)}, f32[3,512]{1,0:T(4,128)S(1)}, f32[3,512]{1,0:T(4,128)S(1)}) all-reduce(f32[3,512]{1,0:T(4,128)S(1)} %get-tuple-element.66, f32[3,512]{1,0:T(4,128)S(1)} %get-tuple-element.65, ...), channel_id=1, replica_groups=mesh['dp'=16,'rep'=2] {'dp','rep'}, use_global_device_ids=true, to_apply=%region_59.60 | all-reduce | flops 6144 | bytes 49152 | tf_op jit(solution)/shard_map/psum | solution.py:98
  723.5 5.5 collective-permute-start.12
  741.3 10.0 fusion.38
  762.4 10.1 fusion.35
  772.6 6.1 multiply_reduce_fusion.6
  778.7 45.5 %all-reduce.16 = (f32[3,512]{1,0:T(4,128)}, f32[3,512]{1,0:T(4,128)}, f32[3,512]{1,0:T(4,128)}, f32[3,512]{1,0:T(4,128)}) all-reduce(f32[3,512]{1,0:T(4,128)} %get-tuple-element.60, f32[3,512]{1,0:T(4,128)} %get-tuple-element.64, f32[3,512]{1,0:T(4,128)} %get-tuple-element.191, ...), channel_id=1, replica_groups=mesh['dp'=16,'rep'=2] {'dp','rep'}, use_global_device_ids=true, to_apply=%region_63.64 | all-reduce | flops 6144 | bytes 49152 | tf_op jit(solution)/shard_map/psum | solution.py:98
  824.3 2.6 fusion.379
  826.8 2.5 fusion.378
  834.9 39.4 %all-reduce.15 = (f32[3,128]{1,0:T(4,128)S(1)}, f32[3,128]{1,0:T(4,128)S(1)}, f32[3,128]{1,0:T(4,128)S(1)}, f32[3,128]{1,0:T(4,128)S(1)}) all-reduce(f32[3,128]{1,0:T(4,128)S(1)} %get-tuple-element.79, f32[3,128]{1,0:T(4,128)S(1)} %get-tuple-element.78, ...), channel_id=1, replica_groups=mesh['dp'=16,'rep'=2] {'dp','rep'}, use_global_device_ids=true, to_apply=%region_67.68 | all-reduce | flops 1536 | bytes 12288 | tf_op jit(solution)/shard_map/psum | solution.py:98
  881.5 40.7 %all-reduce.14 = (f32[1,512]{1,0:T(1,128)S(1)}, f32[1,512]{1,0:T(1,128)S(1)}, f32[1,512]{1,0:T(1,128)S(1)}, f32[1,512]{1,0:T(1,128)S(1)}) all-reduce(f32[1,512]{1,0:T(1,128)S(1)} %bitcast.957, f32[1,512]{1,0:T(1,128)S(1)} %bitcast.956, f32[1,512]{1,0:T(1,128)S(1)} %bitcast.953, ...), channel_id=1, replica_groups=mesh['dp'=16,'rep'=2] {'dp','rep'}, use_global_device_ids=true, to_apply=%region_72.73 | all-reduce | flops 2048 | bytes 16384 | tf_op jit(solution)/shard_map/psum | solution.py:98
  925.9 3.1 fusion.331
  929.2 6.8 bitcast_add_fusion.1
  938.7 5.5 collective-permute-start.20
  946.2 2.4 collective-permute-done.21
  950.8 4.1 multiply_reduce_fusion.19
  956.6 51.9 %all-reduce.13 = (f32[1,512]{1,0:T(1,128)S(1)}, f32[1,512]{1,0:T(1,128)S(1)}, f32[1,512]{1,0:T(1,128)S(1)}, f32[1,512]{1,0:T(1,128)S(1)}) all-reduce(f32[1,512]{1,0:T(1,128)S(1)} %bitcast.959, f32[1,512]{1,0:T(1,128)S(1)} %bitcast.958, f32[1,512]{1,0:T(1,128)S(1)} %bitcast.955, ...), channel_id=1, replica_groups=mesh['dp'=16,'rep'=2] {'dp','rep'}, use_global_device_ids=true, to_apply=%region_76.77 | all-reduce | flops 2048 | bytes 16384 | tf_op jit(solution)/shard_map/psum | solution.py:98
  1011.3 3.3 fusion.333
  1014.6 5.1 bitcast_add_fusion.2
  1020.8 15.0 fusion.1
  1035.8 23.8 %bitcast_add_fusion = f32[3,9,512,512]{3,2,1,0:T(8,128)} fusion(f32[3,9,512,512,1]{3,2,4,1,0:T(8,128)} %fusion.1, bf16[3,9,16,16,512]{4,3,2,0,1:T(8,128)(2,1)} %copy-done.83, bf16[3,16,16,512]{3,2,1,0:T(8,128)(2,1)S(1)} %copy-done.5), kind=kOutput, calls=%fused_computation | convolution fusion | flops 3630956544 | bytes 64487424 | tf_op jit(solution)/shard_map/knrwc,krwd->kncd/dot_general | solution.py:222
  1061.5 2.1 reshape.638
  1063.6 2.1 reshape.642
  1066.9 2.7 reduce_sum.578
  1073.4 2.4 fusion.45
  1075.8 126.3 %all-reduce.34 = bf16[3,512,128]{2,0,1:T(4,128)(2,1)S(1)} all-reduce(f32[3,512,128]{2,0,1:T(4,128)S(1)} %copy.129), channel_id=9, replica_groups=mesh['dp'=16,'rep'=2] {'dp'}, use_global_device_ids=true, to_apply=%region_104.105.clone | all-reduce | flops 196608 | bytes 1179648
  1206.1 8.7 collective-permute-start.16
  1228.3 149.8 %reduce-scatter.5.cloned.1.call-done = f32[3,3,32,512]{3,2,0,1:T(8,128)} async-done(((f32[3,3,512,512]{3,2,0,1:T(8,128)}), f32[3,3,32,512]{3,2,0,1:T(8,128)}) %reduce-scatter.5.cloned.1.call-update) | async-done | bytes 589840 | tf_op jit(solution)/shard_map/reduce_scatter | solution.py:277
  1379.9 581.4 %reduce-scatter.11.cloned.1.call-done = f32[3,3,3,32,512]{4,3,2,1,0:T(8,128)} async-done(((f32[3,3,3,512,512]{4,3,2,1,0:T(8,128)}), f32[3,3,3,32,512]{4,3,2,1,0:T(8,128)}) %reduce-scatter.11.cloned.1.call-update) | async-done | bytes 1769488 | tf_op jit(solution)/shard_map/reduce_scatter | solution.py:281
  1961.3 2.5 convert_element_type.270
  1965.5 4.5 fusion.73
  1970.0 4.5 fusion.85
  1975.5 71.2 %reduce-scatter.9.cloned.1.call-done = f32[3,8,512]{2,1,0:T(8,128)} async-done(((f32[3,128,512]{2,1,0:T(8,128)}), f32[3,8,512]{2,1,0:T(8,128)}) %reduce-scatter.9.cloned.1.call-update) | async-done | bytes 49168 | tf_op jit(solution)/shard_map/reduce_scatter | solution.py:280
  2047.5 3.6 all-reduce.28
  2052.4 14.4 all-reduce.33.cloned.1.call-done
  (644 shorter events, 173.9 us)
Async XLA Ops:
  7.2 106.9 %copy-start.163 = (f32[2,512]{1,0:T(2,128)S(1)}, f32[2,512]{1,0:T(2,128)}, u32[]{:S(2)}) copy-start(f32[2,512]{1,0:T(2,128)} %param.27) | copy-start | bytes 12292
  7.2 108.3 %copy-start.54 = (bf16[3,2,8,8,512]{4,3,2,1,0:T(8,128)(2,1)S(1)}, bf16[3,2,8,8,512]{4,3,2,1,0:T(8,128)(2,1)}, u32[]{:S(2)}) copy-start(bf16[3,2,8,8,512]{4,3,2,1,0:T(8,128)(2,1)} %param.35) | copy-start | bytes 1179652
  7.2 125.0 %all-gather.4.cloned.1.call-start = ((), (), s32[]{:S(2)}) async-start(), calls=%async_computation.4 | async-start | bytes 5013504 | tf_op jit(solution)/shard_map/all_gather | solution.py:155
  8.0 241.4 %all-gather.6.cloned.1.call-start = ((), (), s32[]{:S(2)}) async-start(), calls=%async_computation.5 | async-start | bytes 5013504 | tf_op jit(solution)/shard_map/all_gather | solution.py:156
  8.7 546.0 %all-gather.8.cloned.1.call-start = ((), (), s32[]{:S(2)}) async-start(), calls=%async_computation.6 | async-start | bytes 15040512 | tf_op jit(solution)/shard_map/all_gather | solution.py:159
  10.9 1000.2 %copy-start.38 = (f32[16,16]{1,0:T(8,128)}, f32[16,16]{1,0:T(8,128)S(1)}, u32[]{:S(2)}) copy-start(f32[16,16]{1,0:T(8,128)S(1)} %get-tuple-element.246) | copy-start | bytes 3076
  11.0 1000.0 %copy-start.40 = (f32[16,16]{1,0:T(8,128)}, f32[16,16]{1,0:T(8,128)S(1)}, u32[]{:S(2)}) copy-start(f32[16,16]{1,0:T(8,128)S(1)} %get-tuple-element.247) | copy-start | bytes 3076
  12.2 110.3 %collective-permute-start.6 = (bf16[1,1,16,512]{3,2,1,0:T(8,128)(2,1)S(1)}, bf16[1,1,16,512]{3,2,1,0:T(8,128)(2,1)S(1)}, u32[]{:S(2)}, u32[]{:S(2)}) collective-permute-start(bf16[1,1,16,512]{3,2,1,0:T(8,128)(2,1)S(1)} %get-tuple-element.185), channel_id=1, source_target_pairs={{0,1},{1,2},{2,3},{3,4},{4,5},{5,6},{6,7},{7,8},{8,9},{9,10},{10,1... | collective-permute-start | bytes 49160 | tf_op jit(solution)/shard_map/ppermute | solution.py:14
  14.6 107.9 %collective-permute-start.7 = (bf16[1,1,16,512]{3,2,1,0:T(8,128)(2,1)S(1)}, bf16[1,1,16,512]{3,2,1,0:T(8,128)(2,1)S(1)}, u32[]{:S(2)}, u32[]{:S(2)}) collective-permute-start(bf16[1,1,16,512]{3,2,1,0:T(8,128)(2,1)S(1)} %get-tuple-element.186), channel_id=1, source_target_pairs={{1,0},{2,1},{3,2},{4,3},{5,4},{6,5},{7,6},{8,7},{9,8},{10,9},{11,1... | collective-permute-start | bytes 49160 | tf_op jit(solution)/shard_map/ppermute | solution.py:17
  15.9 106.4 %collective-permute-start = (bf16[1,1,16,512]{3,2,1,0:T(8,128)(2,1)S(1)}, bf16[1,1,16,512]{3,2,1,0:T(8,128)(2,1)S(1)}, u32[]{:S(2)}, u32[]{:S(2)}) collective-permute-start(bf16[1,1,16,512]{3,2,1,0:T(8,128)(2,1)S(1)} %get-tuple-element.187), channel_id=1, source_target_pairs={{0,1},{1,2},{2,3},{3,4},{4,5},{5,6},{6,7},{7,8},{8,9},{9,10},{10,1... | collective-permute-start | bytes 49160 | tf_op jit(solution)/shard_map/ppermute | solution.py:14
  21.0 101.3 %collective-permute-start.1 = (bf16[1,1,16,512]{3,2,1,0:T(8,128)(2,1)S(1)}, bf16[1,1,16,512]{3,2,1,0:T(8,128)(2,1)S(1)}, u32[]{:S(2)}, u32[]{:S(2)}) collective-permute-start(bf16[1,1,16,512]{3,2,1,0:T(8,128)(2,1)S(1)} %get-tuple-element.188), channel_id=1, source_target_pairs={{1,0},{2,1},{3,2},{4,3},{5,4},{6,5},{7,6},{8,7},{9,8},{10,9},{11,1... | collective-permute-start | bytes 49160 | tf_op jit(solution)/shard_map/ppermute | solution.py:17
  22.3 1204.1 %reduce-scatter.7.cloned.1.call-start = ((), (), s32[]{:S(2)}) async-start(), calls=%async_computation.8 | async-start | bytes 10027008 | tf_op jit(solution)/shard_map/reduce_scatter | solution.py:278
  72.7 279.5 %copy-start.34 = (bf16[3,512,128]{2,1,0:T(8,128)(2,1)}, bf16[3,512,128]{2,1,0:T(8,128)(2,1)S(1)}, u32[]{:S(2)}) copy-start(bf16[3,512,128]{2,1,0:T(8,128)(2,1)S(1)} %all_gather.22) | copy-start | bytes 1179652
  112.6 325.0 %copy-start.36 = (bf16[3,128,512]{2,1,0:T(8,128)(2,1)}, bf16[3,128,512]{2,1,0:T(8,128)(2,1)S(1)}, u32[]{:S(2)}) copy-start(bf16[3,128,512]{2,1,0:T(8,128)(2,1)S(1)} %all_gather.23) | copy-start | bytes 1179652
  114.0 128.2 %copy-start.66 = (bf16[16]{0:T(256)(128)(2,1)}, bf16[16]{0:T(256)(128)(2,1)S(1)}, u32[]{:S(2)}) copy-start(bf16[16]{0:T(256)(128)(2,1)S(1)} %get-tuple-element.244) | copy-start | bytes 100
  114.0 133.0 %copy-start.74 = (bf16[16]{0:T(256)(128)(2,1)}, bf16[16]{0:T(256)(128)(2,1)S(1)}, u32[]{:S(2)}) copy-start(bf16[16]{0:T(256)(128)(2,1)S(1)} %get-tuple-element.243) | copy-start | bytes 100
  114.1 126.0 %copy-start.62 = (bf16[16]{0:T(256)(128)(2,1)}, bf16[16]{0:T(256)(128)(2,1)S(1)}, u32[]{:S(2)}) copy-start(bf16[16]{0:T(256)(128)(2,1)S(1)} %get-tuple-element.250) | copy-start | bytes 100
  114.1 132.8 %copy-start.70 = (bf16[16]{0:T(256)(128)(2,1)}, bf16[16]{0:T(256)(128)(2,1)S(1)}, u32[]{:S(2)}) copy-start(bf16[16]{0:T(256)(128)(2,1)S(1)} %get-tuple-element.249) | copy-start | bytes 100
  114.1 112.5 %copy-start.139 = (f32[1,512]{1,0:T(1,128)}, f32[1,512]{1,0:T(1,128)S(1)}, u32[]{:S(2)}) copy-start(f32[1,512]{1,0:T(1,128)S(1)} %get-tuple-element.228) | copy-start | bytes 6148
  114.1 236.4 %copy-start.159 = (f32[1,512]{1,0:T(1,128)}, f32[1,512]{1,0:T(1,128)S(1)}, u32[]{:S(2)}) copy-start(f32[1,512]{1,0:T(1,128)S(1)} %get-tuple-element.227) | copy-start | bytes 6148
  136.9 89.8 %copy-start.26 = (f32[16,16,512]{2,1,0:T(8,128)}, f32[16,16,512]{2,1,0:T(8,128)S(1)}, u32[]{:S(2)}) copy-start(f32[16,16,512]{2,1,0:T(8,128)S(1)} %get-tuple-element.254) | copy-start | bytes 1572868
  136.9 87.9 %copy-start.161 = (f32[2,512]{1,0:T(2,128)S(1)}, f32[2,512]{1,0:T(2,128)}, u32[]{:S(2)}) copy-start(f32[2,512]{1,0:T(2,128)} %param.26) | copy-start | bytes 12292
  140.1 99.8 %copy-start.28 = (f32[16,16,512]{2,1,0:T(8,128)}, f32[16,16,512]{2,1,0:T(8,128)S(1)}, u32[]{:S(2)}) copy-start(f32[16,16,512]{2,1,0:T(8,128)S(1)} %get-tuple-element.252) | copy-start | bytes 1572868
  227.2 9.7 collective-permute-start.8
  228.5 8.4 collective-permute-start.9
  229.8 7.2 collective-permute-start.2
  235.4 4.3 collective-permute-start.3
  254.1 96.5 %copy-start.32 = (f32[16,16,512]{2,1,0:T(8,128)}, f32[16,16,512]{2,1,0:T(8,128)S(1)}, u32[]{:S(2)}) copy-start(f32[16,16,512]{2,1,0:T(8,128)S(1)} %get-tuple-element.256) | copy-start | bytes 1572868
  257.3 93.6 %copy-start.30 = (f32[16,16,512]{2,1,0:T(8,128)}, f32[16,16,512]{2,1,0:T(8,128)S(1)}, u32[]{:S(2)}) copy-start(f32[16,16,512]{2,1,0:T(8,128)S(1)} %get-tuple-element.258) | copy-start | bytes 1572868
  525.9 9.5 collective-permute-start.4
  527.2 8.2 collective-permute-start.5
  528.5 7.5 collective-permute-start.10
  534.1 4.4 collective-permute-start.11
  581.0 87.5 %copy-start.96 = (f32[3,512]{1,0:T(4,128)S(1)}, f32[3,512]{1,0:T(4,128)}, u32[]{:S(2)}) copy-start(f32[3,512]{1,0:T(4,128)} %param.32) | copy-start | bytes 18436
  581.0 88.7 %copy-start.98 = (f32[16,16]{1,0:T(8,128)S(1)}, f32[16,16]{1,0:T(8,128)}, u32[]{:S(2)}) copy-start(f32[16,16]{1,0:T(8,128)} %fusion.348) | copy-start | bytes 3076
  581.0 88.7 %copy-start.99 = (f32[16,16]{1,0:T(8,128)S(1)}, f32[16,16]{1,0:T(8,128)}, u32[]{:S(2)}) copy-start(f32[16,16]{1,0:T(8,128)} %fusion.346) | copy-start | bytes 3076
  581.0 88.7 %copy-start.128 = (f32[3,512]{1,0:T(4,128)S(1)}, f32[3,512]{1,0:T(4,128)}, u32[]{:S(2)}) copy-start(f32[3,512]{1,0:T(4,128)} %param.33) | copy-start | bytes 18436
  720.3 10.0 collective-permute-start.18
  721.6 8.7 collective-permute-start.19
  723.5 27.9 %collective-permute-start.12 = (bf16[3,1,16,512]{3,2,1,0:T(8,128)(2,1)S(1)}, bf16[3,1,16,512]{3,2,1,0:T(8,128)(2,1)S(1)}, u32[]{:S(2)}, u32[]{:S(2)}) collective-permute-start(bf16[3,1,16,512]{3,2,1,0:T(8,128)(2,1)S(1)} %get-tuple-element.161), channel_id=1, source_target_pairs={{0,1},{1,2},{2,3},{3,4},{4,5},{5,6},{6,7},{7,8},{8,9},{9,10},{10,1... | collective-permute-start | bytes 147464 | tf_op jit(solution)/shard_map/ppermute | solution.py:14
  729.0 22.4 %collective-permute-start.13 = (bf16[3,1,16,512]{3,2,1,0:T(8,128)(2,1)S(1)}, bf16[3,1,16,512]{3,2,1,0:T(8,128)(2,1)S(1)}, u32[]{:S(2)}, u32[]{:S(2)}) collective-permute-start(bf16[3,1,16,512]{3,2,1,0:T(8,128)(2,1)S(1)} %get-tuple-element.162), channel_id=1, source_target_pairs={{1,0},{2,1},{3,2},{4,3},{5,4},{6,5},{7,6},{8,7},{9,8},{10,9},{11,1... | collective-permute-start | bytes 147464 | tf_op jit(solution)/shard_map/ppermute | solution.py:17
  936.0 442.1 %reduce-scatter.5.cloned.1.call-start = ((), (), s32[]{:S(2)}) async-start(), calls=%async_computation.7 | async-start | bytes 10027008 | tf_op jit(solution)/shard_map/reduce_scatter | solution.py:277
  936.1 9.9 collective-permute-start.14
  937.4 8.6 collective-permute-start.15
  938.7 7.4 collective-permute-start.20
  944.3 4.3 collective-permute-start.21
  1019.7 941.6 %reduce-scatter.11.cloned.1.call-start = ((), (), s32[]{:S(2)}) async-start(), calls=%async_computation.10 | async-start | bytes 30081024 | tf_op jit(solution)/shard_map/reduce_scatter | solution.py:281
  1059.7 987.1 %reduce-scatter.9.cloned.1.call-start = ((), (), s32[]{:S(2)}) async-start(), calls=%async_computation.9 | async-start | bytes 835584 | tf_op jit(solution)/shard_map/reduce_scatter | solution.py:280
  1073.3 128.9 %copy-start.146 = (f32[1,512]{1,0:T(1,128)S(1)}, f32[1,512]{1,0:T(1,128)}, u32[]{:S(2)}) copy-start(f32[1,512]{1,0:T(1,128)} %copy-done.145) | copy-start | bytes 6148
  1073.3 128.9 %copy-start.148 = (f32[1,512]{1,0:T(1,128)S(1)}, f32[1,512]{1,0:T(1,128)}, u32[]{:S(2)}) copy-start(f32[1,512]{1,0:T(1,128)} %copy-done.147) | copy-start | bytes 6148
  1073.3 128.9 %copy-start.154 = (f32[1,512]{1,0:T(1,128)S(1)}, f32[1,512]{1,0:T(1,128)}, u32[]{:S(2)}) copy-start(f32[1,512]{1,0:T(1,128)} %copy-done.153) | copy-start | bytes 6148
  1073.4 128.9 %copy-start.156 = (f32[1,512]{1,0:T(1,128)S(1)}, f32[1,512]{1,0:T(1,128)}, u32[]{:S(2)}) copy-start(f32[1,512]{1,0:T(1,128)} %copy-done.155) | copy-start | bytes 6148
  1073.4 132.1 %copy-start.16 = (bf16[16,16,512]{2,1,0:T(8,128)(2,1)S(1)}, bf16[16,16,512]{2,1,0:T(8,128)(2,1)}, u32[]{:S(2)}) copy-start(bf16[16,16,512]{2,1,0:T(8,128)(2,1)} %copy-done.15) | copy-start | bytes 786436
  1073.4 132.1 %copy-start.142 = (f32[1,512]{1,0:T(1,128)S(1)}, f32[1,512]{1,0:T(1,128)}, u32[]{:S(2)}) copy-start(f32[1,512]{1,0:T(1,128)} %copy-done.141) | copy-start | bytes 6148
  1073.4 132.1 %copy-start.144 = (f32[1,512]{1,0:T(1,128)S(1)}, f32[1,512]{1,0:T(1,128)}, u32[]{:S(2)}) copy-start(f32[1,512]{1,0:T(1,128)} %copy-done.143) | copy-start | bytes 6148
  1073.4 132.1 %copy-start.150 = (f32[1,512]{1,0:T(1,128)S(1)}, f32[1,512]{1,0:T(1,128)}, u32[]{:S(2)}) copy-start(f32[1,512]{1,0:T(1,128)} %copy-done.149) | copy-start | bytes 6148
  1073.4 132.1 %copy-start.152 = (f32[1,512]{1,0:T(1,128)S(1)}, f32[1,512]{1,0:T(1,128)}, u32[]{:S(2)}) copy-start(f32[1,512]{1,0:T(1,128)} %copy-done.151) | copy-start | bytes 6148
  1073.4 143.1 %copy-start.77 = (bf16[16]{0:T(256)(128)(2,1)S(1)}, bf16[16]{0:T(256)(128)(2,1)}, u32[]{:S(2)}) copy-start(bf16[16]{0:T(256)(128)(2,1)} %copy-done.74) | copy-start | bytes 100
  1202.2 864.6 %all-reduce.33.cloned.1.call-start = ((), (), s32[]{:S(2)}) async-start(), calls=%async_computation.11 | async-start | bytes 2949120 | tf_op jit(solution)/shard_map/psum | solution.py:285
  1202.9 13.5 collective-permute-start.22
  1204.2 12.2 collective-permute-start.23
  1206.1 11.1 collective-permute-start.16
  1214.8 4.3 collective-permute-start.17
  1379.9 585.6 %copy-start.39 = (f32[16,16]{1,0:T(8,128)S(1)}, f32[16,16]{1,0:T(8,128)}, u32[]{:S(2)}) copy-start(f32[16,16]{1,0:T(8,128)} %copy-done.38) | copy-start | bytes 3076
  (140 other events, 2320.6 us)
Sparse Core Ops, SparseCore 0:
  10.8 92.7 all-gather.3
  106.4 79.3 all-gather.5
  188.6 169.6 all-gather.7
  936.2 226.7 reduce-scatter.6
  1165.1 212.9 reduce-scatter.4
  1380.3 581.0 reduce-scatter.10
  1963.6 83.0 reduce-scatter.8
  2050.0 16.7 all-reduce.32
where the time goes:
time: 2090 us; the launch traced here: 2080 us
  blocking collectives  854 us (41%)
  waiting for transfers between devices  828 us (40%)
  matrix products  139 us (7%)
  other arithmetic  127 us (6%)
  starting transfers between devices  61.5 us (3%)
  local copies, waits for them, and re-layouts  51.2 us (2%)
    reduce_scatter x1, waiting for transfers between devices, local(): lax.psum_scatter(weight_grad_task, 'dp', scatter_dimension=3, tiled=True)  581 us
    psum x5, blocking collectives, normalize_back(): lax.psum((jnp.sum(grad_out * valid_mask, axis=(1, 2)), jnp.sum(grad_out *...  217 us
    psum x5, blocking collectives, normalize(): lax.psum((jnp.sum(masked, axis=(1, 2)), local_count), ('dp', 'rep'))  214 us
    psum x5, blocking collectives, normalize(): spread = lax.psum(jnp.sum(centered * centered, axis=(1, 2)), ('dp', 'rep'))  206 us
    reduce_scatter x1, waiting for transfers between devices, local(): lax.psum_scatter(weight_grad_one, 'dp', scatter_dimension=2, tiled=True)  150 us
    unnamed x1, blocking collectives  126 us
    reduce_scatter x1, waiting for transfers between devices, local(): lax.psum_scatter(weight_grad_expand, 'dp', scatter_dimension=1, tiled=True)  71.2 us
    all_gather x1, blocking collectives, local(): lax.all_gather(squeeze, 'dp', axis=1, tiled=True)  47.7 us
  transfers between devices with their start and end apart: 32, of which 8 were waited for; matrix products, arithmetic and copies ran while one was open for 10% of the time, Pallas kernels for 0%

commit v1 on v0

v1 whole, which is shorter than its diff:
```python
import functools
import math

import jax
import jax.numpy as jnp
from jax import lax
from jax.experimental import pallas as pl
from jax.experimental.pallas import tpu as pltpu
from jax.sharding import PartitionSpec as P

EPSILON = 1e-05
AXES = ("dp", "rep")
F32 = jnp.float32
BF16 = jnp.bfloat16
BLOCKS = 16
NEAR = 256 * 1024
FAR = 750000
SPARE = 8 * 1024 * 1024


class Sizes:
    def __init__(self, batches, rows, cols, channels, tasks):
        self.batches, self.rows, self.cols, self.channels = batches, rows, cols, channels
        self.tasks = tasks
        self.own = rows * cols
        self.ext = (rows + 2) * cols
        self.half = channels // 2
        self.block = channels // BLOCKS


def whole(_=None):
    return pl.BlockSpec(memory_space=pltpu.VMEM)


def scalars():
    return pl.BlockSpec(memory_space=pltpu.SMEM)


def in_place():
    return pl.BlockSpec(memory_space=pltpu.HBM)


def unread():
    return pl.BlockSpec(memory_space=pl.ANY)


def per_task(*shape):
    return pl.BlockSpec((1, *shape), lambda t: (t, *(0 for _ in shape)))


def row_of(index, size):
    return pl.ds(pl.multiple_of(index * size, size), size)


def columns_of(s):
    return lax.broadcasted_iota(jnp.int32, (s.cols, s.channels), 0)


def width_at(tab, s, m, i):
    return tab[m * (s.rows + 2) + i]


def link_at(tab, s, m, r):
    return tab[s.batches * (s.rows + 2) + m * (s.rows + 1) + r].astype(F32)


def logistic(v):
    return 0.5 + 0.5 * jnp.tanh(0.5 * v)


def silu_slope(v):
    q = logistic(v)
    return q * (1.0 + v * (1.0 - q))


class Norm:
    def __init__(self, coef, back, m, batches):
        self.mean = coef[pl.ds(m, 1), :]
        self.inverse = coef[pl.ds(batches + m, 1), :]
        self.gain = coef[pl.ds(2 * batches + m, 1), :]
        self.shift = coef[pl.ds(3 * batches + m, 1), :]
        if back is not None:
            self.back_shift = back[pl.ds(m, 1), :]
            self.back_gain = back[pl.ds(batches + m, 1), :]

    def scaled(self, z):
        return (z - self.mean) * self.inverse

    def level(self, scaled):
        return self.gain * scaled + self.shift

    def grad(self, dy, scaled):
        return self.gain * self.inverse * (dy - self.back_shift - scaled * self.back_gain)


def stage(s, x_ref, up, own, down):
    col = columns_of(s)
    for m in range(s.batches):

        def put(i, x, m=m):
            at = ext_slice(s, m, i)
            before = jnp.where(col > 0, pltpu.roll(x, 1, 0), 0.0)
            behind = jnp.where(col < s.cols - 1, pltpu.roll(x, s.cols - 1, 0), 0.0)
            x_ref[at, : s.channels] = before.astype(BF16)
            x_ref[at, s.channels : 2 * s.channels] = x.astype(BF16)
            x_ref[at, 2 * s.channels :] = behind.astype(BF16)

        put(0, up(m))
        put(s.rows + 1, down(m))

        def middle(r, m=m, put=put):
            put(r + 1, own(m, r))

        by_groups(s.rows, middle)


def by_groups(count, body):
    size = 4 if count % 4 == 0 else 2

    def step(i, carry):
        for j in range(size):
            body(size * i + j)
        return carry

    lax.fori_loop(0, count // size, step, 0)


def own_slice(s, m, r):
    return pl.ds(pl.multiple_of(m * s.own + r * s.cols, s.cols), s.cols)


def ext_slice(s, m, i):
    return pl.ds(pl.multiple_of(m * s.ext + i * s.cols, s.cols), s.cols)


def each_row(s, body):
    for m in range(s.batches):
        by_groups(s.rows, functools.partial(body, m))


def span_of(s):
    return s.batches * s.ext - 2 * s.cols


def product(s, x_ref, w_ref, p_ref, flipped):
    def part(a, carry):
        rows = pl.ds(pl.multiple_of(a * s.cols, s.cols), span_of(s))
        if flipped:
            total = None
            for b in range(3):
                term = lax.dot_general(
                    x_ref[rows, b * s.channels : (b + 1) * s.channels],
                    w_ref[8 - (3 * a + b)],
                    (((1,), (1,)), ((), ())),
                    preferred_element_type=F32,
                )
                total = term if total is None else total + term
        else:
            taps = w_ref[pl.ds(3 * a, 3)].reshape(3 * s.channels, s.channels)
            total = jnp.dot(x_ref[rows, :], taps, preferred_element_type=F32)
        p_ref[a] = total
        return carry

    lax.fori_loop(0, 3, part, 0)


def combined(s, tab, p_ref, m, r):
    at = ext_slice(s, m, r)
    up, down = link_at(tab, s, m, r), link_at(tab, s, m, r + 1)
    return p_ref[1, at, :] + up * p_ref[0, at, :] + down * p_ref[2, at, :]


def put_statistics(s, tab, load, st_ref):
    col = columns_of(s)
    zero = jnp.zeros((s.cols, s.channels), F32)
    for m in range(s.batches):
        first = width_at(tab, s, m, 1)
        start = jnp.sum(jnp.where(col < first, load(m, 0), 0.0), axis=0, keepdims=True)
        center = start / first.astype(F32)

        def step(i, totals, m=m, center=center):
            for r in (2 * i, 2 * i + 1):
                off = jnp.where(col < width_at(tab, s, m, r + 1), load(m, r) - center, 0.0)
                totals = (totals[0] + off, totals[1] + off * off)
            return totals

        totals = lax.fori_loop(0, s.rows // 2, step, (zero, zero))
        total = jnp.sum(totals[0], axis=0, keepdims=True)
        spread = jnp.sum(totals[1], axis=0, keepdims=True)
        count = first
        for r in range(1, s.rows):
            count = count + width_at(tab, s, m, r + 1)
        count = count.astype(F32)
        st_ref[pl.ds(m, 1), :] = total + count * center
        st_ref[pl.ds(s.batches + m, 1), :] = jnp.maximum(spread - total * total / count, 0.0)


def put_gradients(s, st_ref, load):
    zero = jnp.zeros((s.cols, s.channels), F32)
    for m in range(s.batches):

        def step(i, totals, m=m):
            for r in (2 * i, 2 * i + 1):
                dy, scaled = load(m, r)
                totals = (totals[0] + dy, totals[1] + dy * scaled)
            return totals

        totals = lax.fori_loop(0, s.rows // 2, step, (zero, zero))
        st_ref[pl.ds(m, 1), :] = jnp.sum(totals[0], axis=0, keepdims=True)
        st_ref[pl.ds(s.batches + m, 1), :] = jnp.sum(totals[1], axis=0, keepdims=True)


def put_edges(s, src_ref, up_ref, down_ref):
    for m in range(s.batches):
        up_ref[pl.ds(m * s.cols, s.cols), :] = src_ref[pl.ds(m * s.own, s.cols), :]
        down_ref[pl.ds(m * s.cols, s.cols), :] = src_ref[
            pl.ds((m + 1) * s.own - s.cols, s.cols), :
        ]


def fetch(s, pieces, slots, w_ref, sem, first, count):
    copies = []
    for piece in pieces:
        for j in range(piece.shape[0]):
            at = len(copies)
            block, half = slots[at], slots[2 * BLOCKS + at // BLOCKS]
            copies.append(
                pltpu.make_async_copy(
                    piece.at[j, pl.ds(first, count)],
                    w_ref.at[:, row_of(block, s.block), row_of(half, s.half)],
                    sem.at[at],
                )
            )
    return copies


def start_all(copies):
    for copy in copies:
        copy.start()


def wait_all(copies):
    for copy in copies:
        copy.wait()


def conv_one_kernel(
    s, tab, slots, img, img_up, img_down, p0, p1, p2, p3, z, st, eu, ed, x, p, w, sem
):
    copies = fetch(s, (p0, p1, p2, p3), slots, w, sem, 0, 9)
    start_all(copies)
    col = columns_of(s)

    def valid(row, m, i):
        return jnp.where(col < width_at(tab, s, m, i), row.astype(F32), 0.0)

    stage(
        s,
        x,
        lambda m: valid(img_up[pl.ds(m * s.cols, s.cols), :], m, 0),
        lambda m, r: valid(img[own_slice(s, m, r), :], m, r + 1),
        lambda m: valid(img_down[pl.ds(m * s.cols, s.cols), :], m, s.rows + 1),
    )
    wait_all(copies)
    convolved(s, tab, x, w, p, z, st, eu, ed)


def convolved(s, tab, x, w, p, z, st, eu, ed):
    product(s, x, w, p, False)

    def row(m, r):
        y = combined(s, tab, p, m, r)
        z[own_slice(s, m, r), :] = y
        return y

    put_statistics(s, tab, row, st)
    put_edges(s, z, eu, ed)


def conv_two_kernel(
    s, tab, slots, z1, zu, zd, coef, p0, p1, z, st, eu, ed, h1, x, p, w, sem
):
    copies = fetch(s, (p0, p1), slots, w, sem, 0, 9)
    start_all(copies)
    col = columns_of(s)
    norms = [Norm(coef, None, m, s.batches) for m in range(s.batches)]

    def active(row, m, i):
        level = norms[m].level(norms[m].scaled(row))
        y = jnp.where(col < width_at(tab, s, m, i), level * logistic(level), 0.0)
        return y.astype(BF16).astype(F32)

    def own(m, r):
        y = active(z1[own_slice(s, m, r), :], m, r + 1)
        h1[own_slice(s, m, r), :] = y.astype(BF16)
        return y

    stage(
        s,
        x,
        lambda m: active(zu[pl.ds(m * s.cols, s.cols), :], m, 0),
        own,
        lambda m: active(zd[pl.ds(m * s.cols, s.cols), :], m, s.rows + 1),
    )
    wait_all(copies)
    convolved(s, tab, x, w, p, z, st, eu, ed)


def squeeze_kernel(s, tab, slots, z2, zu, zd, coef, p0, p1, shared, a, st, low, w, sem):
    copies = fetch(s, (p0, p1), slots, w, sem, 9, 1)
    start_all(copies)
    col = columns_of(s)
    for m in range(s.batches):
        norm = Norm(coef, None, m, s.batches)

        def active(x, i, m=m, norm=norm):
            level = norm.level(norm.scaled(x))
            y = jnp.where(col < width_at(tab, s, m, i), level * logistic(level), 0.0)
            shared[ext_slice(s, m, i), :] = y
            low[ext_slice(s, m, i), :] = y.astype(BF16)

        active(zu[pl.ds(m * s.cols, s.cols), :], 0)
        active(zd[pl.ds(m * s.cols, s.cols), :], s.rows + 1)

        def step(r, m=m, active=active):
            active(z2[own_slice(s, m, r), :], r + 1)

        by_groups(s.rows, step)
    wait_all(copies)
    a[...] = jnp.dot(low[...], w[0], preferred_element_type=F32)
    put_statistics(s, tab, lambda m, r: a[ext_slice(s, m, r + 1), :], st)


def lane_task(s, shape, dim):
    return (lax.broadcasted_iota(jnp.int32, shape, dim) // 8) % 4


def expand_kernel(s, tab, slots, a, coef, p0, p1, e, st, narrow, low, w, sem):
    t = pl.program_id(0)
    copies = fetch(s, (p0, p1), slots, w, sem, 10, 1)

    @pl.when(t == 0)
    def _():
        start_all(copies)
        col = columns_of(s)
        for m in range(s.batches):
            norm = Norm(coef, None, m, s.batches)

            def step(i, m=m, norm=norm):
                level = norm.level(norm.scaled(a[ext_slice(s, m, i), :]))
                y = jnp.where(col < width_at(tab, s, m, i), level * logistic(level), 0.0)
                low[ext_slice(s, m, i), :] = y.astype(BF16)

            by_groups(s.rows + 2, step)
            narrow[pl.ds(m * s.own, s.own), :] = low[pl.ds(m * s.ext + s.cols, s.own), :]
        wait_all(copies)

    mine = lane_task(s, (s.batches * s.ext, s.channels), 1) == t
    chosen = jnp.where(mine, low[...].astype(F32), 0.0).astype(BF16)
    e[0] = jnp.dot(chosen, w[0], preferred_element_type=F32)
    put_statistics(s, tab, lambda m, r: e[0, ext_slice(s, m, r + 1), :], st.at[0])


def task_kernel(
    s, tab, slots, e, shared, coef, *refs
):
    pieces, (k, st, eu, ed, gated, x, p, w, sem) = refs[:-9], refs[-9:]
    t = pl.program_id(0)

    def copies(task):
        return fetch(s, pieces, slots, w.at[task % 2], sem.at[task % 2], 9 * task, 9)

    @pl.when(t == 0)
    def _():
        start_all(copies(0))

    @pl.when(t + 1 < s.tasks)
    def _():
        start_all(copies(t + 1))

    col = columns_of(s)
    norms = [Norm(coef.at[0], None, m, s.batches) for m in range(s.batches)]

    def active(m, i):
        level = norms[m].level(norms[m].scaled(e[0, ext_slice(s, m, i), :]))
        att = jnp.where(col < width_at(tab, s, m, i), logistic(level), 0.0)
        return (att * shared[ext_slice(s, m, i), :]).astype(BF16).astype(F32)

    def own(m, r):
        y = active(m, r + 1)
        gated[0, own_slice(s, m, r), :] = y.astype(BF16)
        return y

    stage(s, x, lambda m: active(m, 0), own, lambda m: active(m, s.rows + 1))
    wait_all(copies(t))
    convolved(s, tab, x, w.at[t % 2], p, k.at[0], st.at[0], eu.at[0], ed.at[0])


def task_slope_kernel(
    s, tab, scale, k, ku, kd, coef, cot, cot_up, cot_down, dl, st, features, pair, line
):
    t = pl.program_id(0)
    factor = 0.25 * scale[t]
    col = columns_of(s)
    norms = [Norm(coef.at[0], None, m, s.batches) for m in range(s.batches)]

    zero = jnp.zeros((s.cols, s.channels), F32)
    few = s.cols // 2

    def spread(half_row):
        value = factor * half_row.astype(F32)
        for c in range(0, s.channels, 128):
            at = c // 128 * s.cols
            line[pl.ds(at, few, stride=2), :] = value[:, c : c + 128]
            line[pl.ds(at + 1, few, stride=2), :] = value[:, c : c + 128]
        return jnp.concatenate(
            [line[row_of(c // 128, s.cols), :] for c in range(0, s.channels, 128)], axis=1
        )

    def slope(x, weight, m, i):
        scaled = norms[m].scaled(x)
        level = norms[m].level(scaled)
        q = logistic(level)
        inside = col < width_at(tab, s, m, i)
        dy = jnp.where(inside, weight * (q * (1.0 + level * (1.0 - q))), 0.0)
        dl[0, ext_slice(s, m, i), :] = dy
        return dy, scaled, jnp.where(inside, level * q, 0.0)

    for m in range(s.batches):
        at, pooled = pl.ds(m * s.cols, s.cols), pl.ds(m * few, few)
        slope(ku[0, at, :], spread(cot_up[0, pooled, :]), m, 0)
        slope(kd[0, at, :], spread(cot_down[0, pooled, :]), m, s.rows + 1)

        def step(i, totals, m=m):
            finished = None
            weight = spread(cot[0, row_of(m * (s.rows // 2) + i, few), :])
            for r in (2 * i, 2 * i + 1):
                dy, scaled, y = slope(k[0, own_slice(s, m, r), :], weight, m, r + 1)
                totals = (totals[0] + dy, totals[1] + dy * scaled)
                finished = y if finished is None else finished + y
            for c in range(0, s.channels, 128):
                pair[row_of(c // 128, s.cols), :] = finished[:, c : c + 128]
            for c in range(0, s.channels, 128):
                even = pair[pl.ds(c // 128 * s.cols, few, stride=2), :]
                odd = pair[pl.ds(c // 128 * s.cols + 1, few, stride=2), :]
                features[0, row_of(m * (s.rows // 2) + i, few), c : c + 128] = 0.25 * (even + odd)
            return totals

        totals = lax.fori_loop(0, s.rows // 2, step, (zero, zero))
        st[0, pl.ds(m, 1), :] = jnp.sum(totals[0], axis=0, keepdims=True)
        st[0, pl.ds(s.batches + m, 1), :] = jnp.sum(totals[1], axis=0, keepdims=True)


def task_back_kernel(
    s, tab, slots, dl, k, ku, kd, coef, back, e, shared, coef_e, *refs
):
    pieces, (dle, part, st, dk, x, p, w, sem) = refs[:-8], refs[-8:]
    t = pl.program_id(0)

    def copies(task):
        return fetch(s, pieces, slots, w.at[task % 2], sem.at[task % 2], 9 * task, 9)

    @pl.when(t == 0)
    def _():
        start_all(copies(0))
        part[...] = jnp.zeros_like(part)

    @pl.when(t + 1 < s.tasks)
    def _():
        start_all(copies(t + 1))

    col = columns_of(s)
    norms = [Norm(coef.at[0], back.at[0], m, s.batches) for m in range(s.batches)]

    def grad(row, m, i):
        dy = dl[0, ext_slice(s, m, i), :]
        dz = norms[m].grad(dy, norms[m].scaled(row))
        dz = jnp.where(col < width_at(tab, s, m, i), dz, 0.0).astype(BF16)
        dk[0, ext_slice(s, m, i), :] = dz
        return dz.astype(F32)

    stage(
        s,
        x,
        lambda m: grad(ku[0, pl.ds(m * s.cols, s.cols), :], m, 0),
        lambda m, r: grad(k[0, own_slice(s, m, r), :], m, r + 1),
        lambda m: grad(kd[0, pl.ds(m * s.cols, s.cols), :], m, s.rows + 1),
    )
    wait_all(copies(t))
    product(s, x, w.at[t % 2], p, True)
    wide = [Norm(coef_e.at[0], None, m, s.batches) for m in range(s.batches)]

    def slope(m, r):
        scaled = wide[m].scaled(e[0, ext_slice(s, m, r + 1), :])
        q = logistic(wide[m].level(scaled))
        att = jnp.where(col < width_at(tab, s, m, r + 1), q, 0.0)
        share = combined(s, tab, p, m, r) * att
        part[own_slice(s, m, r), :] += share
        dy = share * shared[ext_slice(s, m, r + 1), :] * (1.0 - q)
        dle[0, own_slice(s, m, r), :] = dy
        return dy, scaled

    put_gradients(s, st.at[0], slope)


def expand_back_kernel(
    s, tab, slots, dle, e, coef_e, back_e, a, coef_a, p0, p1, da, st, de, w, sem
):
    t = pl.program_id(0)
    copies = fetch(s, (p0, p1), slots, w, sem, 10, 1)

    @pl.when(t == 0)
    def _():
        start_all(copies)

    col = columns_of(s)
    norms = [Norm(coef_e.at[0], back_e.at[0], m, s.batches) for m in range(s.batches)]

    def grad(m, r):
        scaled = norms[m].scaled(e[0, ext_slice(s, m, r + 1), :])
        dz = norms[m].grad(dle[0, own_slice(s, m, r), :], scaled)
        dz = jnp.where(col < width_at(tab, s, m, r + 1), dz, 0.0)
        de[0, own_slice(s, m, r), :] = dz.astype(BF16)

    each_row(s, grad)

    @pl.when(t == 0)
    def _():
        wait_all(copies)
        da[...] = jnp.zeros_like(da)

    term = lax.dot_general(de[0], w[0], (((1,), (1,)), ((), ())), preferred_element_type=F32)
    mine = lane_task(s, (1, s.channels), 1) == t
    da[...] += jnp.where(mine, term, 0.0)

    @pl.when(t == s.tasks - 1)
    def _():
        narrow = [Norm(coef_a, None, m, s.batches) for m in range(s.batches)]

        def slope(m, r):
            scaled = narrow[m].scaled(a[ext_slice(s, m, r + 1), :])
            dy = da[own_slice(s, m, r), :] * silu_slope(narrow[m].level(scaled))
            dy = jnp.where(col < width_at(tab, s, m, r + 1), dy, 0.0)
            da[own_slice(s, m, r), :] = dy
            return dy, scaled

        put_gradients(s, st, slope)


def squeeze_back_kernel(
    s, tab, slots, dla, a, coef_a, back_a, part, z2, coef, p0, p1, dl, st, eu, ed, da, w, sem
):
    copies = fetch(s, (p0, p1), slots, w, sem, 9, 1)
    start_all(copies)
    col = columns_of(s)
    narrow = [Norm(coef_a, back_a, m, s.batches) for m in range(s.batches)]

    def grad(m, r):
        scaled = narrow[m].scaled(a[ext_slice(s, m, r + 1), :])
        dz = narrow[m].grad(dla[own_slice(s, m, r), :], scaled)
        dz = jnp.where(col < width_at(tab, s, m, r + 1), dz, 0.0)
        da[own_slice(s, m, r), :] = dz.astype(BF16)

    each_row(s, grad)
    wait_all(copies)
    dl[...] = lax.dot_general(da[...], w[0], (((1,), (1,)), ((), ())), preferred_element_type=F32)
    norms = [Norm(coef, None, m, s.batches) for m in range(s.batches)]

    def slope(m, r):
        at = own_slice(s, m, r)
        scaled = norms[m].scaled(z2[at, :])
        dy = (dl[at, :] + part[at, :]) * silu_slope(norms[m].level(scaled))
        dy = jnp.where(col < width_at(tab, s, m, r + 1), dy, 0.0)
        dl[at, :] = dy
        return dy, scaled

    put_gradients(s, st, slope)
    put_edges(s, dl, eu, ed)


def norm_rows(s, tab, dl, dlu, dld, z, zu, zd, coef, back, dz):
    col = columns_of(s)
    norms = [Norm(coef, back, m, s.batches) for m in range(s.batches)]

    def grad(dy, x, m, i):
        y = norms[m].grad(dy, norms[m].scaled(x))
        y = jnp.where(col < width_at(tab, s, m, i), y, 0.0).astype(BF16)
        dz[ext_slice(s, m, i), :] = y
        return y.astype(F32)

    def up(m):
        at = pl.ds(m * s.cols, s.cols)
        return grad(dlu[at, :], zu[at, :], m, 0)

    def down(m):
        at = pl.ds(m * s.cols, s.cols)
        return grad(dld[at, :], zd[at, :], m, s.rows + 1)

    def own(m, r):
        at = own_slice(s, m, r)
        return grad(dl[at, :], z[at, :], m, r + 1)

    return up, own, down


def kept_rows(s, dz):
    def row(m, i):
        return dz[ext_slice(s, m, i), :].astype(F32)

    return (lambda m: row(m, 0)), (lambda m, r: row(m, r + 1)), (lambda m: row(m, s.rows + 1))


def conv_two_back_kernel(
    s, tab, slots, dl, dlu, dld, z, zu, zd, coef, back, z1, coef1, p0, p1, dl1, st, eu, ed, dz, x, p, w, sem
):
    copies = fetch(s, (p0, p1), slots, w, sem, 0, 9)
    start_all(copies)
    stage(s, x, *norm_rows(s, tab, dl, dlu, dld, z, zu, zd, coef, back, dz))
    wait_all(copies)
    product(s, x, w, p, True)
    col = columns_of(s)
    norms = [Norm(coef1, None, m, s.batches) for m in range(s.batches)]

    def slope(m, r):
        scaled = norms[m].scaled(z1[own_slice(s, m, r), :])
        dy = combined(s, tab, p, m, r) * silu_slope(norms[m].level(scaled))
        dy = jnp.where(col < width_at(tab, s, m, r + 1), dy, 0.0)
        dl1[own_slice(s, m, r), :] = dy
        return dy, scaled

    put_gradients(s, st, slope)
    put_edges(s, dl1, eu, ed)


def conv_one_back_kernel(s, tab, slots, dz, p0, p1, p2, p3, out, x, p, w, sem):
    copies = fetch(s, (p0, p1, p2, p3), slots, w, sem, 0, 9)
    start_all(copies)
    stage(s, x, *kept_rows(s, dz))
    wait_all(copies)
    product(s, x, w, p, True)
    col = columns_of(s)

    def mask(m, r):
        y = combined(s, tab, p, m, r)
        out[own_slice(s, m, r), :] = jnp.where(col < width_at(tab, s, m, r + 1), y, 0.0)

    each_row(s, mask)


def put_blocks(s, slots, res, side, keep, send, tap):
    target = (keep, send)[side]
    for block in range(BLOCKS):
        rows = res[block * s.block : (block + 1) * s.block]
        target[slots[(2 + side) * BLOCKS + 2 + block], tap] = rows.astype(BF16)


def put_turned(lanes, v, vt):
    turned = v.T
    vt[0] = turned * lanes[pl.ds(0, 1), :].astype(BF16)
    vt[1] = turned
    vt[2] = turned * lanes[pl.ds(1, 1), :].astype(BF16)


def tap_products(s, slots, vt, x, keep, send):
    def one(tap, carry):
        a, b = 2 - tap // 3, 2 - tap % 3
        for side in (1, 0):
            half = row_of(2 * b + slots[2 * BLOCKS + side], s.half)
            res = None
            for m in range(s.batches):
                rows = pl.ds(pl.multiple_of(m * s.ext + a * s.cols, s.cols), s.own)
                term = jnp.dot(
                    vt[a, :, m * s.own : (m + 1) * s.own],
                    x[rows, half],
                    preferred_element_type=F32,
                )
                res = term if res is None else res + term
            put_blocks(s, slots, res, side, keep, send, tap)
        return carry

    lax.fori_loop(0, 9, one, 0)


def task_weight_kernel(s, slots, lanes, v, dz, keep, send, x, vt):
    stage(s, x, *kept_rows(s, dz.at[0]))
    put_turned(lanes, v[0], vt)
    tap_products(s, slots, vt, x, keep, send)


def conv_two_weight_kernel(
    s, slots, lanes, v, dz, shared, da, narrow, de, keep, send, x, vt
):
    stage(s, x, *kept_rows(s, dz))
    put_turned(lanes, v[...], vt)
    tap_products(s, slots, vt, x, keep, send)
    for m in range(s.batches):
        own = shared[pl.ds(m * s.ext + s.cols, s.own), :].astype(BF16)
        vt[0, :, m * s.own : (m + 1) * s.own] = own.T
    vt[1] = narrow[...].T
    owner = lane_task(s, (s.channels, s.half), 0)
    for side in (1, 0):
        half = row_of(slots[2 * BLOCKS + side], s.half)
        res = jnp.dot(vt[0], da[:, half], preferred_element_type=F32)
        put_blocks(s, slots, res, side, keep, send, 9)
        res = jnp.zeros((s.channels, s.half), F32)
        for t in range(s.tasks):
            term = jnp.dot(vt[1], de[t, :, half], preferred_element_type=F32)
            res = jnp.where(owner == t, term, res)
        put_blocks(s, slots, res, side, keep, send, 10)


def conv_one_weight_kernel(
    s, tab, slots, lanes, img, dl, dlu, dld, z, zu, zd, coef, back, keep, send, dz, x, v, vt
):
    stage(s, x, *norm_rows(s, tab, dl, dlu, dld, z, zu, zd, coef, back, dz))
    col = columns_of(s)

    def valid(m, r):
        at = own_slice(s, m, r)
        row = jnp.where(col < width_at(tab, s, m, r + 1), img[at, :].astype(F32), 0.0)
        v[at, :] = row.astype(BF16)

    each_row(s, valid)
    put_turned(lanes, v[...], vt)
    tap_products(s, slots, vt, x, keep, send)


def is_near(x, spec):
    return spec.memory_space == pltpu.VMEM and x.size * x.dtype.itemsize <= NEAR


def block_bytes(x, spec):
    if spec.block_shape is None:
        return x.size * x.dtype.itemsize if spec.memory_space == pltpu.VMEM else 0
    return 2 * math.prod(spec.block_shape) * x.dtype.itemsize


def is_far(x, spec, grid):
    if spec.memory_space == pltpu.HBM:
        return True
    part = spec.block_shape is not None and math.prod(spec.block_shape) < x.size
    return grid == (1,) and part and x.size > FAR


def placed(x, spec, grid):
    if is_far(x, spec, grid):
        return pltpu.with_memory_space_constraint(x, pltpu.HBM)
    return pltpu.with_memory_space_constraint(x, pltpu.VMEM) if is_near(x, spec) else x


def placed_shape(x, spec):
    return pltpu.VMEM(x.shape, x.dtype) if is_near(x, spec) else x


def call(kernel, s, ins, outs, scratch, grid=None, after=()):
    shapes = [shape for shape, _ in outs]
    given, extra = len(ins), len(after)

    def body(*refs):
        kernel(s, *refs[:given], *refs[given + extra :])

    ins = [(placed(x, spec, grid), spec) for x, spec in ins] + [(x, unread()) for x in after]
    options = {} if grid is None else {"grid": grid}
    room = sum(block_bytes(x, spec) for x, spec in list(ins) + list(outs))
    for ref in scratch:
        if ref.memory_space == pltpu.VMEM:
            room += math.prod(ref.shape) * jnp.dtype(ref.dtype).itemsize
    return pl.pallas_call(
        body,
        out_shape=[placed_shape(x, spec) for x, spec in outs],
        in_specs=[spec for _, spec in ins],
        out_specs=[spec for _, spec in outs],
        scratch_shapes=scratch,
        compiler_params=pltpu.CompilerParams(vmem_limit_bytes=room + SPARE),
        cost_estimate=pl.CostEstimate(flops=1024, bytes_accessed=1024, transcendentals=0),
        **options,
    )(*[x for x, _ in ins])


class Links:
    def __init__(self, dp, rep):
        self.dp, self.rep, self.count = dp, rep, dp * rep
        self.me_dp, self.me_rep = lax.axis_index("dp"), lax.axis_index("rep")
        self.me = self.me_dp * rep + self.me_rep
        bits = (self.count - 1).bit_length()
        self.groups = [(1,)]
        for bit in range(1, bits, 2):
            low = 1 << bit
            self.groups.append((low,) if bit + 1 == bits else (low, 2 * low, 3 * low))
        self.direct = dp == BLOCKS and rep == 2
        self.column = ((16, 16), (8, 8), (24, 24))
        self.steps = ((4, 2), (2, 4))
        self.ring = list(range(dp))
        if self.direct:
            self.ring = [
                4 * (z if i % 2 == 0 else 3 - z) + column
                for i, column in enumerate((0, 1, 3, 2))
                for z in range(4)
            ]

    def swap(self, x, masks):
        pairs = [(i, i ^ masks[i % 2]) for i in range(self.count)]
        return lax.ppermute(x, AXES, pairs)

    def shift(self, x, by):
        pairs = [(i, i + by) for i in range(self.count) if 0 <= i + by < self.count]
        return lax.ppermute(x, AXES, pairs)

    def neighbours(self, top, bottom):
        return self.shift(bottom, 1), self.shift(top, -1)


def total_of(items):
    if len(items) == 2:
        return items[0] + items[1]
    return (items[0] + items[1]) + (items[2] + items[3])


def group_counts(links, counts):
    places = jnp.arange(links.count, dtype=jnp.int32)[None, :]

    def among(place, low):
        same = (places | low) == (place | low)
        return jnp.sum(jnp.where(same, counts, 0.0), axis=1, keepdims=True)

    return [
        [among(links.me ^ mask, group[0] - 1) for mask in (0, *group)] for group in links.groups
    ]


def statistics_over(links, st, stages, batches, gain, shift):
    tasks, _, channels = st.shape
    given = []
    for group, counts in zip(links.groups, stages):
        met = [st] + [links.swap(st, (mask, mask)) for mask in group]
        count = total_of(counts)
        total = total_of([x[:, :batches] for x in met])
        mean = total / count
        spread = total_of(
            [x[:, batches:] + n * (x[:, :batches] / n - mean) ** 2 for x, n in zip(met, counts)]
        )
        st = jnp.concatenate([total, spread], axis=1)
        given.append(st)
    mean = st[:, :batches] / count
    inverse = lax.rsqrt(st[:, batches:] / count + EPSILON)
    wide = (tasks, batches, channels)
    coef = jnp.concatenate(
        [
            mean,
            inverse,
            jnp.broadcast_to(gain[:, None], wide),
            jnp.broadcast_to(shift[:, None], wide),
        ],
        axis=1,
    )
    return coef, given


def sums_over(links, st, between=None):
    given = []
    for i, group in enumerate(links.groups):
        st = total_of([st] + [links.swap(st, (mask, mask)) for mask in group])
        given.append(st)
        if i == 1 and between is not None:
            extra = between(given)
            st = tied(st, extra) if extra else st
    return st, given


def join_kernel(s, *refs):
    at = 0
    for ref in refs[:-1]:
        refs[-1][pl.ds(at, ref.shape[0])] = ref[...]
        at += ref.shape[0]


def tied(x, after):
    count = len(after)
    return pl.pallas_call(
        lambda *refs: None,
        out_shape=jax.ShapeDtypeStruct(x.shape, x.dtype),
        in_specs=[unread()] * (1 + count),
        out_specs=unread(),
        input_output_aliases={0: 0},
    )(x, *after)


def joined(arrays, after=()):
    shape = (sum(x.shape[0] for x in arrays), *arrays[0].shape[1:])
    return call(
        join_kernel,
        None,
        [(x, whole()) for x in arrays],
        [(jax.ShapeDtypeStruct(shape, arrays[0].dtype), whole())],
        [],
        after=after,
    )[0]


class Gather:
    def __init__(self, links, block, after_z=()):
        self.links = links
        half = block.shape[2] // 2
        mine = lax.dynamic_slice_in_dim(block, links.me_rep * half, half, axis=2)[None]
        self.own = joined([mine], after_z) if after_z else mine
        self.along = [links.swap(self.own, masks) for masks in links.column]

    def across(self, after=()):
        self.four = joined([self.own, *self.along], after)
        self.fourth = self.links.swap(self.four, self.links.steps[0])
        return self.four

    def finish(self, after=()):
        links = self.links
        self.mine = joined([self.four, self.fourth], after)
        self.more = links.swap(self.mine, links.steps[1])
        self.pieces = [
            self.mine,
            self.more,
            links.swap(self.mine, (1, 1)),
            links.swap(self.more, (1, 1)),
        ]
        return self.mine


def gather_halves(links, block, order):
    half = block.shape[2] // 2
    mine = lax.dynamic_slice_in_dim(block, links.me_rep * half, half, axis=2)
    return lax.all_gather(mine, "dp", axis_index_groups=order)


def split_blocks(full, parts):
    slabs, rows, cols = full.shape
    x = full.reshape(slabs, BLOCKS, rows // BLOCKS, 2, cols // 2)
    x = jnp.transpose(x, (3, 1, 0, 2, 4))
    size = BLOCKS // parts
    return [x[side, i * size : (i + 1) * size] for side in range(2) for i in range(parts)]


def slot_table(links):
    places = jnp.arange(BLOCKS, dtype=jnp.int32)
    if not links.direct:
        return jnp.concatenate([places, places, jnp.array([0, 1], jnp.int32), places, places])
    tables = []
    for core in range(2):
        offsets = [0] + [masks[core] // 2 for masks in links.column]
        for masks in links.steps:
            offsets = offsets + [o ^ (masks[core] // 2) for o in offsets]
        tables.append(offsets)
    inverse = [[t.index(o) for o in range(BLOCKS)] for t in tables]
    first = links.me_rep == 0
    me = links.me_dp
    ours = jnp.where(first, jnp.array(tables[0], jnp.int32), jnp.array(tables[1], jnp.int32))
    theirs = jnp.where(first, jnp.array(tables[1], jnp.int32), jnp.array(tables[0], jnp.int32))
    back = [jnp.array(t, jnp.int32) for t in inverse]
    offset = me ^ places
    match = (offset[:, None] == places[None, :]).astype(jnp.int32)
    slot = [
        jnp.sum(match * jnp.where(first, back[i], back[1 - i])[None, :], axis=1) for i in range(2)
    ]
    halves = jnp.stack([links.me_rep, 1 - links.me_rep]).astype(jnp.int32)
    return jnp.concatenate([me ^ ours, me ^ theirs, halves, *slot]).astype(jnp.int32)


def fold_kernel(s, *refs):
    total = refs[0][...].astype(F32)
    for ref in refs[1:-1]:
        total = total + ref[...].astype(F32)
    refs[-1][...] = total.astype(BF16)


class Scatter:
    def __init__(self, links, keep, send):
        self.links, self.keep, self.send = links, keep, send
        self.parts, self.count = [keep], BLOCKS
        if links.direct:
            self.got = ()
        else:
            self.full = join_blocks(keep, send)
            self.got = ()

    def start(self, after=()):
        if self.links.direct:
            send = tied(self.send, after) if after else self.send
            self.parts.append(self.links.swap(send, (1, 1)))
        return self

    def step(self, after=()):
        links = self.links
        if not links.direct:
            return ()
        self.count //= 2
        count, shape = self.count, self.keep.shape[1:]
        (out,) = call(
            fold_kernel,
            None,
            [(part, pl.BlockSpec((count, *shape), lambda i: (1, 0, 0, 0))) for part in self.parts],
            [
                (
                    jax.ShapeDtypeStruct((count, *shape), BF16),
                    pl.BlockSpec((count, *shape), lambda i: (0, 0, 0, 0)),
                )
            ],
            [],
            grid=(1,),
            after=after,
        )
        self.got = (links.swap(out, links.steps[1 if count == 8 else 0]),)
        self.parts.extend(self.got)
        return (out,)


def column_kernel(s, *refs, counts):
    ins, outs = refs[:-4], refs[-4:]
    first, at = 0, 0
    for count in counts:
        slabs = ins[first].shape[1]
        for i, out in enumerate(outs):
            total = None
            for ref in ins[first : first + count]:
                term = ref[i].astype(F32)
                total = term if total is None else total + term
            out[pl.ds(at, slabs)] = total.astype(out.dtype)
        first, at = first + count, at + slabs


class Column:
    def __init__(self, links, units, after=()):
        self.links = links
        block = units[0].keep.shape[2:]
        slabs = sum(unit.keep.shape[1] for unit in units)
        ins = []
        for unit in units:
            spec = pl.BlockSpec((4, *unit.keep.shape[1:]), lambda i: (0, 0, 0, 0))
            ins.extend((part, spec) for part in unit.parts)
        spec = pl.BlockSpec((slabs, *block), lambda i: (0, 0, 0))
        kinds = (F32, BF16, BF16, BF16)
        self.own, *self.out = call(
            functools.partial(column_kernel, counts=[len(unit.parts) for unit in units]),
            None,
            ins,
            [(jax.ShapeDtypeStruct((slabs, *block), kind), spec) for kind in kinds],
            [],
            grid=(1,),
            after=after,
        )
        self.got = [links.swap(x, masks) for x, masks in zip(self.out, links.column)]

    def rows(self, after=()):
        mine = tied(self.own, after) if after else self.own
        for part in self.got:
            mine = mine + part.astype(F32)
        return join_halves(self.links, mine)


def join_halves(links, mine):
    other = links.swap(mine, (1, 1)).astype(F32)
    mine = mine.astype(F32)
    first = links.me_rep == 0
    return jnp.concatenate(
        [jnp.where(first, mine, other), jnp.where(first, other, mine)], axis=-1
    )


def join_blocks(keep, send):
    x = jnp.concatenate([keep, send], axis=-1).astype(F32)
    x = jnp.transpose(x, (1, 0, 2, 3))
    return x.reshape(x.shape[0], x.shape[1] * x.shape[2], x.shape[3])


def summed_shard(x, dim):
    return lax.psum(lax.psum_scatter(x, "dp", scatter_dimension=dim, tiled=True), "rep")


def bottleneck_row(x, channels):
    tasks, width = x.shape
    x = x.reshape(tasks, width // 8, 8)
    x = jnp.pad(x, ((0, channels // width - tasks), (0, 0), (0, 0)))
    return jnp.transpose(x, (1, 0, 2)).reshape(1, channels)


def bottleneck_lanes(x, channels):
    tasks, rows, width = x.shape
    x = x.reshape(tasks, rows, width // 8, 8)
    x = jnp.pad(x, ((0, channels // width - tasks), (0, 0), (0, 0), (0, 0)))
    return jnp.transpose(x, (1, 2, 0, 3)).reshape(rows, channels)


def lanes_to_tasks(x, tasks):
    rows, channels = x.shape
    x = x.reshape(rows, channels // 32, 4, 8)[:, :, :tasks]
    return jnp.transpose(x, (2, 0, 1, 3)).reshape(tasks, rows, channels // 4)


def tables(lengths, widths, offset, rows, total, cols):
    ends = 2 * jnp.cumsum(lengths, axis=1)
    starts = ends - 2 * lengths

    def width_of(places):
        before = (places[None, :, None] < ends[:, None, :]) & (
            places[None, :, None] >= starts[:, None, :]
        )
        return jnp.sum(before.astype(jnp.int32) * widths[:, None, :], axis=2)

    near = offset - 1 + jnp.arange(rows + 2, dtype=jnp.int32)
    below = offset + jnp.arange(rows + 1, dtype=jnp.int32)
    first = jnp.sum((below[None, :, None] == starts[:, None, :]).astype(jnp.int32), axis=2)
    tab = jnp.concatenate([width_of(near).reshape(-1), (1 - first).reshape(-1)])
    linked = (1 - first).astype(F32)
    lanes = jnp.stack([linked[:, :-1], linked[:, 1:]])
    lanes = jnp.repeat(lanes, cols, axis=2).reshape(2, -1)
    return tab, lanes, width_of(jnp.arange(total, dtype=jnp.int32))


def local(
    dp,
    rep,
    images,
    lengths,
    widths,
    conv_one,
    conv_two,
    squeeze,
    expand,
    task_conv,
    gains_shared,
    biases_shared,
    gains_squeeze,
    biases_squeeze,
    gains_expand,
    biases_expand,
    gains_task,
    biases_task,
    loss_history,
    cotangent,
):
    batches, rows, cols, channels = images.shape
    tasks = cotangent.shape[0]
    s = Sizes(batches, rows, cols, channels, tasks)
    links = Links(dp, rep)
    pixels, edge = batches * s.own, batches * cols
    ext = batches * s.ext

    def f32(*shape):
        return jax.ShapeDtypeStruct(shape, F32)

    def b16(*shape):
        return jax.ShapeDtypeStruct(shape, BF16)

    slots = slot_table(links)
    places = jnp.arange(BLOCKS, dtype=jnp.int32)
    ring = jnp.array(links.ring, jnp.int32) if links.direct else places
    halves = slots[2 * BLOCKS : 2 * BLOCKS + 2]
    plain = jnp.concatenate([places, places, halves])
    around = jnp.concatenate([ring, ring, halves])
    shard = conv_one.shape[2]
    if links.direct:
        narrow_rows = bottleneck_lanes(squeeze, channels)[None]
        wide_rows = jnp.pad(
            expand.reshape(-1, channels), ((0, shard - tasks * expand.shape[1]), (0, 0))
        )[None]
        two_mine = gather_halves(
            links,
            jnp.concatenate([conv_two.reshape(9, shard, channels), narrow_rows, wide_rows], axis=0),
            None,
        )
        task_rows = task_conv.reshape(9 * tasks, shard, channels)
        task_mine = gather_halves(links, task_rows, [links.ring])
        first = Gather(links, conv_one.reshape(9, shard, channels))
        first.across()
        first.finish()
        one = first.pieces
    else:
        full = lax.all_gather(conv_one, "dp", axis=2, tiled=True)
        one = split_blocks(full.reshape(9, channels, channels), 2)
        full = lax.all_gather(conv_two, "dp", axis=2, tiled=True).reshape(9, channels, channels)
        narrow_rows = bottleneck_lanes(lax.all_gather(squeeze, "dp", axis=1, tiled=True), channels)
        wide_rows = lax.all_gather(expand, "dp", axis=1, tiled=True)
        wide_rows = bottleneck_lanes(jnp.transpose(wide_rows, (0, 2, 1)), channels).T
        two = split_blocks(jnp.concatenate([full, narrow_rows[None], wide_rows[None]], axis=0), 1)
        full = lax.all_gather(task_conv, "dp", axis=3, tiled=True)
        three = split_blocks(full.reshape(9 * tasks, channels, channels), 1)

    tab, lanes, all_widths = tables(lengths, widths, links.me * rows, rows, links.count * rows, cols)
    counts = jnp.sum(all_widths.reshape(batches, links.count, rows).astype(F32), axis=2)
    stages = group_counts(links, counts)
    pixel_count = jnp.sum(counts, axis=1, keepdims=True)
    twice_count = jnp.concatenate([pixel_count, pixel_count], axis=0)
    loss_ratio = loss_history[:, 1] / loss_history[:, 0]
    task_scale = tasks * jax.nn.softmax(loss_ratio / 2.0)

    img = images.reshape(pixels, channels)
    img_up, img_down = links.neighbours(
        images[:, 0].reshape(edge, channels), images[:, -1].reshape(edge, channels)
    )
    cot_up, cot_down = links.neighbours(cotangent[:, :, :1], cotangent[:, :, -1:])
    cot = cotangent.reshape(tasks, pixels // 4, channels)
    cot_up, cot_down = (x.reshape(tasks, edge // 2, channels) for x in (cot_up, cot_down))

    pieces = [in_place()] * 4
    span = span_of(s)
    shifts = pltpu.VMEM((ext, 3 * channels), BF16)
    sums = pltpu.VMEM((3, span, channels), F32)
    weights = pltpu.VMEM((9, channels, channels), BF16)
    matrix = pltpu.VMEM((1, channels, channels), BF16)
    sems = pltpu.SemaphoreType.DMA((2 * BLOCKS,))

    def sync(st, gain, shift):
        return statistics_over(links, st, stages, batches, gain, shift)

    st_shape, edge_shape = f32(2 * batches, channels), f32(edge, channels)

    z1, st, eu, ed = call(
        conv_one_kernel,
        s,
        [(tab, scalars()), (slots, scalars()), (img, whole()), (img_up, whole()), (img_down, whole())]
        + list(zip(one, pieces)),
        [(f32(pixels, channels), whole()), (st_shape, whole()), (edge_shape, whole()), (edge_shape, whole())],
        [shifts, sums, weights, sems],
    )
    z1_up, z1_down = links.neighbours(eu, ed)
    coef1, given = sync(st[None], gains_shared[0:1], biases_shared[0:1])
    coef1 = coef1[0]
    if links.direct:
        two_mine = tied(two_mine, (given[-1],))
        two = [two_mine, links.swap(two_mine, (1, 1))]

    z2, st, eu, ed, hidden = call(
        conv_two_kernel,
        s,
        [(tab, scalars()), (plain, scalars())]
        + [(x, whole()) for x in (z1, z1_up, z1_down, coef1)]
        + list(zip(two, pieces)),
        [(f32(pixels, channels), whole()), (st_shape, whole()), (edge_shape, whole()), (edge_shape, whole()), (b16(pixels, channels), whole())],
        [shifts, sums, weights, sems],
        after=(cot_up, cot_down),
    )
    z2_up, z2_down = links.neighbours(eu, ed)
    coef2, _ = sync(st[None], gains_shared[1:2], biases_shared[1:2])
    coef2 = coef2[0]

    shared, a, st = call(
        squeeze_kernel,
        s,
        [(tab, scalars()), (plain, scalars())]
        + [(x, whole()) for x in (z2, z2_up, z2_down, coef2)]
        + list(zip(two, pieces)),
        [(f32(ext, channels), whole()), (f32(ext, channels), whole()), (st_shape, whole())],
        [pltpu.VMEM((ext, channels), BF16), matrix, sems],
    )
    coef_a, _ = sync(
        st[None], bottleneck_row(gains_squeeze, channels), bottleneck_row(biases_squeeze, channels)
    )
    coef_a = coef_a[0]

    grid = (tasks,)
    whole_task = functools.partial(
        lambda *shape: pl.BlockSpec(shape, lambda t: tuple(0 for _ in shape))
    )
    ext_task, own_task, edge_task = (
        per_task(ext, channels),
        per_task(pixels, channels),
        per_task(edge, channels),
    )
    st_task, coef_task = per_task(2 * batches, channels), per_task(4 * batches, channels)
    ext_all, own_all = whole_task(ext, channels), whole_task(pixels, channels)
    st_all, coef_all = whole_task(2 * batches, channels), whole_task(4 * batches, channels)
    edge_all = whole_task(edge, channels)

    e, st, narrow = call(
        expand_kernel,
        s,
        [(tab, scalars()), (plain, scalars()), (a, ext_all), (coef_a, coef_all)]
        + list(zip(two, pieces)),
        [(f32(tasks, ext, channels), ext_task), (f32(tasks, 2 * batches, channels), st_task), (b16(pixels, channels), own_all)],
        [pltpu.VMEM((ext, channels), BF16), matrix, sems],
        grid=grid,
    )
    coef_e, given = sync(st, gains_expand, biases_expand)
    if links.direct:
        task_mine = tied(task_mine, (given[1],))
        three = [task_mine, links.swap(task_mine, (1, 1))]

    pair = [shifts, sums, pltpu.VMEM((2, 9, channels, channels), BF16), pltpu.SemaphoreType.DMA((2, 2 * BLOCKS))]
    k, st, eu, ed, gated = call(
        task_kernel,
        s,
        [(tab, scalars()), (around, scalars()), (e, ext_task), (shared, ext_all), (coef_e, coef_task)]
        + [(x, in_place()) for x in three],
        [
            (f32(tasks, pixels, channels), own_task),
            (f32(tasks, 2 * batches, channels), st_task),
            (f32(tasks, edge, channels), edge_task),
            (f32(tasks, edge, channels), edge_task),
            (b16(tasks, pixels, channels), own_task),
        ],
        pair,
        grid=grid,
    )
    k_up, k_down = links.neighbours(eu, ed)
    coef_k, _ = sync(st, gains_task, biases_task)

    dlk, st, pooled = call(
        task_slope_kernel,
        s,
        [(tab, scalars()), (task_scale, scalars()), (k, own_task), (k_up, edge_task), (k_down, edge_task), (coef_k, coef_task), (cot, per_task(pixels // 4, channels)), (cot_up, per_task(edge // 2, channels)), (cot_down, per_task(edge // 2, channels))],
        [
            (f32(tasks, ext, channels), ext_task),
            (f32(tasks, 2 * batches, channels), st_task),
            (f32(tasks, pixels // 4, channels), per_task(pixels // 4, channels)),
        ],
        [pltpu.VMEM((channels // 128 * cols, 128), F32)] * 2,
        grid=grid,
    )
    sums_k, _ = sums_over(links, st)
    back_k = sums_k / twice_count

    dle, part, st, dk = call(
        task_back_kernel,
        s,
        [
            (tab, scalars()),
            (around, scalars()),
            (dlk, ext_task),
            (k, own_task),
            (k_up, edge_task),
            (k_down, edge_task),
            (coef_k, coef_task),
            (back_k, st_task),
            (e, ext_task),
            (shared, ext_all),
            (coef_e, coef_task),
        ]
        + [(x, in_place()) for x in three],
        [
            (f32(tasks, pixels, channels), own_task),
            (f32(pixels, channels), own_all),
            (f32(tasks, 2 * batches, channels), st_task),
            (b16(tasks, ext, channels), ext_task),
        ],
        pair,
        grid=grid,
    )
    sums_e, given = sums_over(links, st)
    back_e = sums_e / twice_count

    def outputs(slabs):
        return b16(BLOCKS, slabs, s.block, s.half)

    turned = pltpu.VMEM((3, channels, pixels), BF16)

    def task_weights(t, after):
        def at(*shape):
            return pl.BlockSpec((1, *shape), lambda i: (t, *(0 for _ in shape)))

        keep, send = call(
            task_weight_kernel,
            s,
            [(slots, scalars()), (lanes, whole_task(2, pixels)), (gated, at(pixels, channels)), (dk, at(ext, channels))],
            [(outputs(9), whole_task(BLOCKS, 9, s.block, s.half))] * 2,
            [shifts, turned],
            grid=(1,),
            after=after,
        )
        return Scatter(links, keep, send)

    task_0 = task_weights(0, (given[0],)).start()
    wait_e = (task_0.keep,)

    dla, st, de = call(
        expand_back_kernel,
        s,
        [
            (tab, scalars()),
            (plain, scalars()),
            (dle, own_task),
            (e, ext_task),
            (coef_e, coef_task),
            (back_e, st_task),
            (a, ext_all),
            (coef_a, coef_all),
        ]
        + list(zip(two, pieces)),
        [(f32(pixels, channels), own_all), (st_shape, st_all), (b16(tasks, pixels, channels), own_task)],
        [matrix, sems],
        grid=grid,
        after=wait_e,
    )
    sums_a, given = sums_over(links, st[None], lambda given: task_0.step((given[1],)))
    sums_a = sums_a[0]
    back_a = sums_a / twice_count
    task_1 = task_weights(1, (given[-1],))
    wait_a = task_0.step((given[-1], task_1.keep))

    dl2, st, eu, ed, da = call(
        squeeze_back_kernel,
        s,
        [(tab, scalars()), (plain, scalars())]
        + [(x, whole()) for x in (dla, a, coef_a, back_a, part, z2, coef2)]
        + list(zip(two, pieces)),
        [(f32(pixels, channels), whole()), (st_shape, whole()), (edge_shape, whole()), (edge_shape, whole()), (b16(pixels, channels), whole())],
        [matrix, sems],
        after=wait_a,
    )
    dl2_up, dl2_down = links.neighbours(eu, ed)
    sums_2, given = sums_over(
        links,
        st[None],
        lambda given: task_1.start((given[0],)).step((given[1], *task_0.got)),
    )
    sums_2 = sums_2[0]
    back_2 = sums_2 / twice_count
    task_2 = task_weights(2, (given[-1],))
    wait_b = task_1.step((given[-1], dl2_up, dl2_down, task_2.keep))

    dl1, st, eu, ed, dz2 = call(
        conv_two_back_kernel,
        s,
        [(tab, scalars()), (plain, scalars())]
        + [(x, whole()) for x in (dl2, dl2_up, dl2_down, z2, z2_up, z2_down, coef2, back_2, z1, coef1)]
        + list(zip(two, pieces)),
        [(f32(pixels, channels), whole()), (st_shape, whole()), (edge_shape, whole()), (edge_shape, whole()), (b16(ext, channels), whole())],
        [shifts, sums, weights, sems],
        after=wait_b,
    )
    dl1_up, dl1_down = links.neighbours(eu, ed)
    sums_1, given = sums_over(
        links,
        st[None],
        lambda given: task_2.start((given[0],)).step((given[1], *task_1.got)),
    )
    sums_1 = sums_1[0]
    back_1 = sums_1 / twice_count

    grad_two = call(
        conv_two_weight_kernel,
        s,
        [(slots, scalars()), (lanes, whole())]
        + [(x, whole()) for x in (hidden, dz2, shared, da, narrow, de)],
        [(outputs(11), whole()), (outputs(11), whole())],
        [shifts, turned],
        after=(given[-1],),
    )
    two_sums = Scatter(links, *grad_two)
    wait_c = task_2.step((given[-1], dl1_up, dl1_down, two_sums.keep))
    two_sums.start(wait_c)
    task_sums = (task_0, task_1, task_2)

    keep, send, dz1 = call(
        conv_one_weight_kernel,
        s,
        [(tab, scalars()), (slots, scalars()), (lanes, whole())]
        + [(x, whole()) for x in (img, dl1, dl1_up, dl1_down, z1, z1_up, z1_down, coef1, back_1)],
        [(outputs(9), whole()), (outputs(9), whole()), (b16(ext, channels), whole())],
        [shifts, pltpu.VMEM((pixels, channels), BF16), turned],
        after=wait_c,
    )
    one_sums = Scatter(links, keep, send)
    wait_d = ()
    if links.direct:
        task_column = Column(links, task_sums, (dz1,))
        one_sums.start(task_column.out[:1])
        wait_d = one_sums.step(two_sums.step(task_column.out))

    (input_grad,) = call(
        conv_one_back_kernel,
        s,
        [(tab, scalars()), (slots, scalars()), (dz1, whole())] + list(zip(one, pieces)),
        [(f32(pixels, channels), whole())],
        [shifts, sums, weights, sems],
        after=wait_d,
    )

    width = squeeze.shape[2]
    if links.direct:
        order = two_sums.step((input_grad,))
        one_sums.step(order)
        last_column = Column(links, (one_sums, two_sums))
        three_rows = task_column.rows()
        last_rows = last_column.rows()
        one_rows, two_rows = last_rows[:9], last_rows[9:]
        grad_squeeze = lanes_to_tasks(two_rows[9], tasks)
        grad_expand = two_rows[10].reshape(4, expand.shape[1], channels)[:tasks]
    else:
        three_rows = summed_shard(jnp.concatenate([part.full for part in task_sums], axis=0), 1)
        full = two_sums.full
        two_rows = summed_shard(full[:9], 1)
        one_rows = summed_shard(one_sums.full, 1)
        grad_squeeze = summed_shard(lanes_to_tasks(full[9], tasks), 1)
        wide = jnp.transpose(lanes_to_tasks(full[10].T, tasks), (0, 2, 1))
        grad_expand = summed_shard(wide, 1)

    def both(sums):
        shift = sum(sums[..., m, :] for m in range(batches))
        gain = sum(sums[..., batches + m, :] for m in range(batches))
        return gain, shift

    gain_1, shift_1 = both(sums_1)
    gain_2, shift_2 = both(sums_2)
    gain_a, shift_a = both(sums_a)
    gain_e, shift_e = both(sums_e)
    gain_k, shift_k = both(sums_k)

    def tasks_row(x):
        return lanes_to_tasks(x[None], tasks).reshape(tasks, width)

    return (
        pooled.reshape(cotangent.shape),
        input_grad.reshape(images.shape),
        one_rows.reshape(conv_one.shape),
        two_rows[:9].reshape(conv_two.shape),
        grad_squeeze,
        grad_expand,
        three_rows.reshape(task_conv.shape),
        jnp.stack([gain_1, gain_2]),
        jnp.stack([shift_1, shift_2]),
        tasks_row(gain_a),
        tasks_row(shift_a),
        gain_e,
        shift_e,
        gain_k,
        shift_k,
    )


def solution(mesh):
    rows = P(None, AXES, None, None)
    pooled = P(None, None, AXES, None, None)
    conv = P(None, None, "dp", None)
    small = P(None, "dp", None)
    task = P(None, None, None, "dp", None)
    rest = P()
    return jax.shard_map(
        functools.partial(local, mesh.shape["dp"], mesh.shape["rep"]),
        mesh=mesh,
        in_specs=(rows, rest, rest, conv, conv, small, small, task) + (rest,) * 9 + (pooled,),
        out_specs=(pooled, rows, conv, conv, small, small, task) + (rest,) * 8,
        check_vma=False,
    )
```

time: 2090 us -> 572 us (0.27)
  blocking collectives: 854 us -> 0 us
  waiting for transfers between devices: 828 us -> 155 us
  Pallas kernels: 0 us -> 145 us
  matrix products: 139 us -> 0 us
  other arithmetic: 127 us -> 24.2 us
  starting transfers between devices: 61.5 us -> 156 us
    reduce_scatter x4 -> x0, waiting for transfers between devices: 802 us -> none  [the longest x1 581 us: local(): lax.psum_scatter(weight_grad_task, 'dp', scatter_dimension=3, tiled=True)]
    psum x16 -> x0, blocking collectives: 640 us -> none  [the longest x5 217 us: normalize_back(): lax.psum((jnp.sum(grad_out * valid_mask, axis=(1, 2)), jnp.sum(grad_out *...]
    pallas_call x0 -> x39, Pallas kernels: none -> 145 us  [the longest x30 145 us: call(): pl.pallas_call(body, out_shape=[placed_shape(x, spec) for x, spec in outs...]
    ppermute x24 -> x116, waiting for transfers between devices: 9.42 us -> 155 us  [the longest x102 150 us: swap(): return lax.ppermute(x, AXES, pairs)]
    dot_general x30 -> x0, matrix products: 139 us -> none  [the longest x2 38.8 us: local(): jnp.einsum('knrwc,krwd->kncd', unfolded_task, task_low, preferred_element...]
    unnamed x1 -> x0, blocking collectives: 126 us -> none
    ppermute x24 -> x116, starting transfers between devices: 61.1 us -> 156 us  [the longest x102 133 us: swap(): return lax.ppermute(x, AXES, pairs)]
    all_gather x2 -> x0, blocking collectives: 87.6 us -> none  [the longest x1 47.7 us: local(): lax.all_gather(squeeze, 'dp', axis=1, tiled=True)]
  transfers between devices with their start and end apart: 32 -> 118, of which waited for: 8 -> 65; matrix products, arithmetic and copies ran while one was open for 10% -> 5% of each run, Pallas kernels for 0% -> 13%
where the time goes in v1:
time: 572 us; the launch traced here: 565 us
  starting transfers between devices  156 us (27%)
  waiting for transfers between devices  155 us (27%)
  Pallas kernels  145 us (25%)
  local copies, waits for them, and re-layouts  67.7 us (12%)
  other arithmetic  24.2 us (4%)
  between operations  16.7 us (3%)
    ppermute x102, waiting for transfers between devices, swap(): return lax.ppermute(x, AXES, pairs)  150 us
    pallas_call x30, Pallas kernels, call(): pl.pallas_call(body, out_shape=[placed_shape(x, spec) for x, spec in outs...  145 us
    ppermute x102, starting transfers between devices, swap(): return lax.ppermute(x, AXES, pairs)  133 us
    unnamed x391, local copies, waits for them, and re-layouts  58.9 us
    ppermute x14, starting transfers between devices, shift(): return lax.ppermute(x, AXES, pairs)  23.1 us
  transfers between devices with their start and end apart: 118, of which 65 were waited for; matrix products, arithmetic and copies ran while one was open for 5% of the time, Pallas kernels for 13%

profile of v1, /device:TPU:0, one launch (start us, length us, event | category | flops | bytes accessed | tf_op | source)
XLA Modules:
  0.0 564.8 jit_solution(3010825926218083912)
XLA Ops:
  11.7 4.1 collective-permute-start.2
  17.4 7.1 %collective-permute-done.2.refs_1_ = bf16[1,9,32,256]{3,2,1,0:T(8,128)(2,1)S(1)} collective-permute-done((bf16[1,9,32,256]{3,2,1,0:T(8,128)(2,1)S(1)}, bf16[1,9,32,256]{3,2,1,0:T(8,128)(2,1)S(1)}, u32[]{:S(2)}, u32[]{:S(2)}) %collective-permute-start.2) | collective-permute-done | bytes 147488 | tf_op jit(solution)/shard_map/ppermute | solution.py:803
  24.4 2.8 collective-permute-done.4.refs_3_
  28.9 8.3 %collective-permute-done.5.refs_1_ = bf16[4,9,32,256]{3,2,1,0:T(8,128)(2,1)S(1)} collective-permute-done((bf16[4,9,32,256]{3,2,1,0:T(8,128)(2,1)S(1)}, bf16[4,9,32,256]{3,2,1,0:T(8,128)(2,1)S(1)}, u32[]{:S(2)}, u32[]{:S(2)}) %collective-permute-start.5) | collective-permute-done | bytes 589856 | tf_op jit(solution)/shard_map/ppermute | solution.py:803
  44.6 14.5 %collective-permute-done.6.refs_6_.refs_4_ = bf16[8,9,32,256]{3,2,1,0:T(8,128)(2,1)} collective-permute-done((bf16[8,9,32,256]{3,2,1,0:T(8,128)(2,1)S(1)}, bf16[8,9,32,256]{3,2,1,0:T(8,128)(2,1)}, u32[]{:S(2)}, u32[]{:S(2)}) %collective-permute-start.6) | collective-permute-done | bytes 1179680 | tf_op jit(solution)/shard_map/ppermute | solution.py:803
  62.3 7.0 %shard_map.354 = (f32[512,512]{1,0:T(8,128)S(1)}, f32[4,512]{1,0:T(4,128)S(1)}, f32[32,512]{1,0:T(8,128)S(1)}, f32[32,512]{1,0:T(8,128)S(1)}) custom-call(s32[70]{0:T(128)S(1)} %pad_add_fusion.refs_0_, s32[66]{0:T(128)S(1)} %concatenate.78.refs_1_.refs_0_, bf16[512,512]{1,0:T(8,128)(2,1)S(1)} %bitcast.109, bf16[32,512]{1,0:T(8,128)(2,1)S(1)} %collective-permute-done.refs_3_, ...), custom_call_target="tpu_custom_call" | custom-call | flops 1024 | bytes 1024 | tf_op jit(solution)/shard_map/pallas_call | solution.py:768
  78.7 3.3 collective-permute-start.15
  89.9 2.4 collective-permute-start.19
  95.1 4.3 collective-permute-start.9
  101.8 7.0 %shard_map.356 = (f32[512,512]{1,0:T(8,128)S(1)}, f32[4,512]{1,0:T(4,128)S(1)}, f32[32,512]{1,0:T(8,128)S(1)}, f32[32,512]{1,0:T(8,128)S(1)}, bf16[512,512]{1,0:T(8,128)(2,1)S(1)}) custom-call(s32[70]{0:T(128)S(1)} %pad_add_fusion.refs_0_, s32[34]{0:T(128)S(1)} %add_add_fusion.17.refs_1_, f32[512,512]{1,0:T(8,128)S(1)} %get-tuple-element.74.refs_2_.refs_10_.refs_7_, ...), custom_call_target="tpu_custom_call" | custom-call | flops 1024 | bytes 1024 | tf_op jit(solution)/shard_map/pallas_call | solution.py:768
  112.1 2.8 collective-permute-start.24
  118.7 2.7 collective-permute-done.26
  128.9 2.4 collective-permute-done.29
  132.2 2.7 shard_map.357
  137.1 3.3 collective-permute-start.30
  143.5 2.9 collective-permute-start.32
  148.1 3.0 collective-permute-done.33
  156.7 2.9 collective-permute-done.36
  162.5 4.4 shard_map.358
  178.0 3.4 collective-permute-start.43
  188.5 2.9 copy-done.126
  193.5 16.6 %shard_map.360 = (f32[3,512,512]{2,1,0:T(8,128)S(1)}, f32[3,4,512]{2,1,0:T(4,128)S(1)}, f32[3,32,512]{2,1,0:T(8,128)S(1)}, f32[3,32,512]{2,1,0:T(8,128)S(1)}, bf16[3,512,512]{2,1,0:T(8,128)(2,1)S(1)}) custom-call(s32[70]{0:T(128)S(1)} %copy-done.107, s32[34]{0:T(128)S(1)} %add_add_fusion.16.refs_1_, ...), custom_call_target="tpu_custom_call" | custom-call | flops 1024 | bytes 1024 | tf_op jit(solution)/shard_map/pallas_call | solution.py:768
  227.9 3.3 collective-permute-done.46.refs_4_.refs_5_
  231.2 4.8 shard_map.361
  236.0 4.2 collective-permute-start.54
  241.0 2.5 collective-permute-start.55
  248.9 2.4 collective-permute-start.59
  253.9 3.0 collective-permute-done.60
  257.6 18.2 %shard_map.362 = (f32[3,512,512]{2,1,0:T(8,128)S(1)}, f32[512,512]{1,0:T(8,128)S(1)}, f32[3,4,512]{2,1,0:T(4,128)}, bf16[3,576,512]{2,1,0:T(8,128)(2,1)S(1)}) custom-call(s32[70]{0:T(128)S(1)} %copy-done.108, s32[34]{0:T(128)S(1)} %add_add_fusion.16.refs_1_, f32[3,576,512]{2,1,0:T(8,128)S(1)} %get-tuple-element.92.refs_2_, ...), custom_call_target="tpu_custom_call" | custom-call | flops 1024 | bytes 1024 | tf_op jit(solution)/shard_map/pallas_call | solution.py:768
  283.9 5.9 %shard_map.363 = (bf16[16,9,32,256]{3,2,1,0:T(8,128)(2,1)S(1)}, bf16[16,9,32,256]{3,2,1,0:T(8,128)(2,1)S(1)}) custom-call(s32[66]{0:T(128)S(1)} %copy-done.115, f32[2,512]{1,0:T(2,128)S(1)} %copy-done.91, bf16[3,512,512]{2,1,0:T(8,128)(2,1)} %copy-done.8, bf16[3,576,512]{2,1,0:T(8,128)(2,1)} %copy-done.7, f32[3,4,512]{2,1,0:T(4,128)S(1)} %add.866.refs_4_), custom_call_target="tpu_custom_call" | custom-call | flops 1024 | bytes 1024 | tf_op jit(solution)/shard_map/pallas_call | solution.py:768
  291.5 2.4 collective-permute-start.64
  296.4 2.9 collective-permute-start.66
  301.1 3.8 collective-permute-done.67
  307.5 5.0 shard_map.364
  321.7 2.9 shard_map.365.refs_1_
  325.3 2.5 collective-permute-start.74
  330.1 3.4 collective-permute-done.75
  335.5 5.9 %shard_map.367 = (bf16[16,9,32,256]{3,2,1,0:T(8,128)(2,1)S(1)}, bf16[16,9,32,256]{3,2,1,0:T(8,128)(2,1)S(1)}) custom-call(s32[66]{0:T(128)S(1)} %copy-done.116, f32[2,512]{1,0:T(2,128)S(1)} %copy-done.92, bf16[3,512,512]{2,1,0:T(8,128)(2,1)} %copy-done.8, bf16[3,576,512]{2,1,0:T(8,128)(2,1)} %copy-done.7, f32[1,4,512]{2,1,0:T(4,128)S(1)} %get-tuple-element.197.refs_4_.refs_3_), custom_call_target="tpu_custom_call" | custom-call | flops 1024 | bytes 1024 | tf_op jit(solution)/shard_map/pallas_call | solution.py:768
  347.2 3.7 shard_map.369
  360.7 5.1 collective-permute-done.81
  367.3 2.9 shard_map.371.refs_1_
  374.1 2.5 collective-permute-start.87
  380.5 5.9 %shard_map.373 = (bf16[16,9,32,256]{3,2,1,0:T(8,128)(2,1)S(1)}, bf16[16,9,32,256]{3,2,1,0:T(8,128)(2,1)S(1)}) custom-call(s32[66]{0:T(128)S(1)} %copy-done.117, f32[2,512]{1,0:T(2,128)S(1)} %copy-done.93, bf16[3,512,512]{2,1,0:T(8,128)(2,1)} %copy-done.8, bf16[3,576,512]{2,1,0:T(8,128)(2,1)} %copy-done.7, f32[1,4,512]{2,1,0:T(4,128)S(1)} %get-tuple-element.195.refs_4_.refs_3_), custom_call_target="tpu_custom_call" | custom-call | flops 1024 | bytes 1024 | tf_op jit(solution)/shard_map/pallas_call | solution.py:768
  390.1 8.2 %shard_map.375 = (f32[512,512]{1,0:T(8,128)S(1)}, f32[4,512]{1,0:T(4,128)S(1)}, f32[32,512]{1,0:T(8,128)}, f32[32,512]{1,0:T(8,128)}, bf16[576,512]{1,0:T(8,128)(2,1)S(1)}) custom-call(s32[70]{0:T(128)S(1)} %copy-done.110, s32[34]{0:T(128)S(1)} %copy-done.124, f32[512,512]{1,0:T(8,128)S(1)} %copy-done.54, ...), custom_call_target="tpu_custom_call" | custom-call | flops 1024 | bytes 1024 | tf_op jit(solution)/shard_map/pallas_call | solution.py:768
  403.5 3.4 collective-permute-start.96
  407.5 2.9 collective-permute-start.94
  410.7 4.3 collective-permute-done.93
  416.5 2.9 shard_map.377.refs_1_
  421.0 2.8 collective-permute-start.98
  438.9 6.5 %shard_map.379 = (bf16[16,11,32,256]{3,2,1,0:T(8,128)(2,1)S(1)}, bf16[16,11,32,256]{3,2,1,0:T(8,128)(2,1)S(1)}) custom-call(s32[66]{0:T(128)S(1)} %copy-done.118, f32[2,512]{1,0:T(2,128)S(1)} %copy-done.94, bf16[512,512]{1,0:T(8,128)(2,1)S(1)} %copy-done.65, bf16[576,512]{1,0:T(8,128)(2,1)S(1)} %copy-done.63, f32[576,512]{1,0:T(8,128)S(1)} %copy-done.17, ...), custom_call_target="tpu_custom_call" | custom-call | flops 1024 | bytes 1024 | tf_op jit(solution)/shard_map/pallas_call | solution.py:768
  445.5 3.0 shard_map.380.refs_12_.refs_1_
  450.4 3.3 collective-permute-start.101
  455.0 5.6 shard_map.381
  463.4 3.2 shard_map.382
  474.5 3.0 shard_map.386.refs_7_
  481.9 2.7 collective-permute-start.113
  485.6 7.7 %shard_map.387.refs_3_ = f32[512,512]{1,0:T(8,128)} custom-call(s32[70]{0:T(128)S(1)} %copy-done.112, s32[66]{0:T(128)S(1)} %copy-done.120, bf16[576,512]{1,0:T(8,128)(2,1)S(1)} %copy-done.44, bf16[8,9,32,256]{3,2,1,0:T(8,128)(2,1)} %copy-done.13, bf16[8,9,32,256]{3,2,1,0:T(8,128)(2,1)} %collective-permute-done.6.refs_6_.refs_4_, ...), custom_call_target="tpu_custom_call" | custom-call | flops 1024 | bytes 1024 | tf_op jit(solution)/shard_map/pallas_call | solution.py:768
  496.7 12.5 %collective-permute-done.104.refs_2_ = bf16[8,9,32,256]{3,2,1,0:T(8,128)(2,1)} collective-permute-done((bf16[8,9,32,256]{3,2,1,0:T(8,128)(2,1)}, bf16[8,9,32,256]{3,2,1,0:T(8,128)(2,1)}, u32[]{:S(2)}, u32[]{:S(2)}) %collective-permute-start.104) | collective-permute-done | bytes 1179680 | tf_op jit(solution)/shard_map/ppermute | solution.py:803
  509.2 2.4 shard_map.389
  516.0 5.8 %collective-permute-done.106.refs_3_ = bf16[4,9,32,256]{3,2,1,0:T(8,128)(2,1)} collective-permute-done((bf16[4,9,32,256]{3,2,1,0:T(8,128)(2,1)}, bf16[4,9,32,256]{3,2,1,0:T(8,128)(2,1)}, u32[]{:S(2)}, u32[]{:S(2)}) %collective-permute-start.106) | collective-permute-done | bytes 589856 | tf_op jit(solution)/shard_map/ppermute | solution.py:803
  521.8 2.9 shard_map.390
  524.7 4.0 collective-permute-start.108
  530.3 14.0 %collective-permute-done.108 = bf16[20,32,256]{2,1,0:T(8,128)(2,1)S(1)} collective-permute-done((bf16[20,32,256]{2,1,0:T(8,128)(2,1)S(1)}, bf16[20,32,256]{2,1,0:T(8,128)(2,1)S(1)}, u32[]{:S(2)}, u32[]{:S(2)}) %collective-permute-start.108) | collective-permute-done | bytes 327712 | tf_op jit(solution)/shard_map/ppermute | solution.py:803
  544.6 7.5 %collective-permute-done.110 = bf16[20,32,256]{2,1,0:T(8,128)(2,1)S(1)} collective-permute-done((bf16[20,32,256]{2,1,0:T(8,128)(2,1)S(1)}, bf16[20,32,256]{2,1,0:T(8,128)(2,1)S(1)}, u32[]{:S(2)}, u32[]{:S(2)}) %collective-permute-start.110) | collective-permute-done | bytes 327712 | tf_op jit(solution)/shard_map/ppermute | solution.py:803
  (746 shorter events, 235.9 us)
Async XLA Ops:
  7.2 81.9 %all-gather.5.cloned.1.call-start = ((), (), s32[]{:S(2)}) async-start(), calls=%async_computation | async-start | bytes 3063808 | tf_op jit(solution)/shard_map/all_gather | solution.py:929
  10.7 166.3 %all-gather.7.cloned.1.call-start = ((), (), s32[]{:S(2)}) async-start(), calls=%async_computation.1 | async-start | bytes 7520256 | tf_op jit(solution)/shard_map/all_gather | solution.py:929
  11.7 12.8 %collective-permute-start.2 = (bf16[1,9,32,256]{3,2,1,0:T(8,128)(2,1)S(1)}, bf16[1,9,32,256]{3,2,1,0:T(8,128)(2,1)S(1)}, u32[]{:S(2)}, u32[]{:S(2)}) collective-permute-start(bf16[1,9,32,256]{3,2,1,0:T(8,128)(2,1)S(1)} %dynamic-slice_bitcast_fusion.refs_0_), channel_id=1, source_target_pairs={{0,16},{1,17},{2,18},{3,19},{4,20},{5,21},{6,22},{7,23},{8,24},{9,... | collective-permute-start | bytes 442376 | tf_op jit(solution)/shard_map/ppermute | solution.py:803
  15.8 8.7 %collective-permute-start.3 = (bf16[1,9,32,256]{3,2,1,0:T(8,128)(2,1)S(1)}, bf16[1,9,32,256]{3,2,1,0:T(8,128)(2,1)S(1)}, u32[]{:S(2)}, u32[]{:S(2)}) collective-permute-start(bf16[1,9,32,256]{3,2,1,0:T(8,128)(2,1)S(1)} %dynamic-slice_bitcast_fusion.refs_0_), channel_id=1, source_target_pairs={{0,8},{1,9},{2,10},{3,11},{4,12},{5,13},{6,14},{7,15},{8,0},{9,1},... | collective-permute-start | bytes 442376 | tf_op jit(solution)/shard_map/ppermute | solution.py:803
  17.4 9.9 %collective-permute-start.4 = (bf16[1,9,32,256]{3,2,1,0:T(8,128)(2,1)S(1)}, bf16[1,9,32,256]{3,2,1,0:T(8,128)(2,1)S(1)}, u32[]{:S(2)}, u32[]{:S(2)}) collective-permute-start(bf16[1,9,32,256]{3,2,1,0:T(8,128)(2,1)S(1)} %dynamic-slice_bitcast_fusion.refs_0_), channel_id=1, source_target_pairs={{0,24},{1,25},{2,26},{3,27},{4,28},{5,29},{6,30},{7,31},{8,16},{9,... | collective-permute-start | bytes 442376 | tf_op jit(solution)/shard_map/ppermute | solution.py:803
  27.3 9.9 %collective-permute-start.5 = (bf16[4,9,32,256]{3,2,1,0:T(8,128)(2,1)S(1)}, bf16[4,9,32,256]{3,2,1,0:T(8,128)(2,1)S(1)}, u32[]{:S(2)}, u32[]{:S(2)}) collective-permute-start(bf16[4,9,32,256]{3,2,1,0:T(8,128)(2,1)S(1)} %shard_map.352.refs_0_), channel_id=1, source_target_pairs={{0,4},{1,3},{2,6},{3,1},{4,0},{5,7},{6,2},{7,5},{8,12},{9,11},{10,... | collective-permute-start | bytes 1769480 | tf_op jit(solution)/shard_map/ppermute | solution.py:803
  37.3 21.8 %collective-permute-start.6 = (bf16[8,9,32,256]{3,2,1,0:T(8,128)(2,1)S(1)}, bf16[8,9,32,256]{3,2,1,0:T(8,128)(2,1)}, u32[]{:S(2)}, u32[]{:S(2)}) collective-permute-start(bf16[8,9,32,256]{3,2,1,0:T(8,128)(2,1)S(1)} %shard_map.353.refs_5_.refs_3_), channel_id=1, source_target_pairs={{0,2},{1,5},{2,0},{3,7},{4,6},{5,1},{6,4},{7,3},{8,10},{9,13},{10,... | collective-permute-start | bytes 3538952 | tf_op jit(solution)/shard_map/ppermute | solution.py:803
  38.9 21.6 %collective-permute-start = (bf16[32,512]{1,0:T(8,128)(2,1)S(1)}, bf16[32,512]{1,0:T(8,128)(2,1)S(1)}, u32[]{:S(2)}, u32[]{:S(2)}) collective-permute-start(bf16[32,512]{1,0:T(8,128)(2,1)S(1)} %bitcast.136), channel_id=1, source_target_pairs={{0,1},{1,2},{2,3},{3,4},{4,5},{5,6},{6,7},{7,8},{8,9},{9,10},{10,1... | collective-permute-start | bytes 98312 | tf_op jit(solution)/shard_map/ppermute | solution.py:807
  40.2 20.3 %collective-permute-start.1 = (bf16[32,512]{1,0:T(8,128)(2,1)S(1)}, bf16[32,512]{1,0:T(8,128)(2,1)S(1)}, u32[]{:S(2)}, u32[]{:S(2)}) collective-permute-start(bf16[32,512]{1,0:T(8,128)(2,1)S(1)} %bitcast.135), channel_id=1, source_target_pairs={{1,0},{2,1},{3,2},{4,3},{5,4},{6,5},{7,6},{8,7},{9,8},{10,9},{11,1... | collective-permute-start | bytes 98312 | tf_op jit(solution)/shard_map/ppermute | solution.py:807
  42.8 17.8 %collective-permute-start.7 = (bf16[8,9,32,256]{3,2,1,0:T(8,128)(2,1)S(1)}, bf16[8,9,32,256]{3,2,1,0:T(8,128)(2,1)}, u32[]{:S(2)}, u32[]{:S(2)}) collective-permute-start(bf16[8,9,32,256]{3,2,1,0:T(8,128)(2,1)S(1)} %shard_map.353.refs_5_.refs_3_), channel_id=1, source_target_pairs={{0,1},{1,0},{2,3},{3,2},{4,5},{5,4},{6,7},{7,6},{8,9},{9,8},{10,11... | collective-permute-start | bytes 3538952 | tf_op jit(solution)/shard_map/ppermute | solution.py:803
  78.7 5.7 %collective-permute-start.15 = (f32[1,4,512]{2,1,0:T(4,128)S(1)}, f32[1,4,512]{2,1,0:T(4,128)S(1)}, u32[]{:S(2)}, u32[]{:S(2)}) collective-permute-start(f32[1,4,512]{2,1,0:T(4,128)S(1)} %pad_maximum_fusion.9), channel_id=1, source_target_pairs={{0,8},{1,9},{2,10},{3,11},{4,12},{5,13},{6,14},{7,15},{8,0},{9,1},... | collective-permute-start | bytes 24584 | tf_op jit(solution)/shard_map/ppermute | solution.py:803
  82.9 5.4 collective-permute-start.17
  89.1 11.1 %collective-permute-start.18 = (bf16[16,11,32,256]{3,2,1,0:T(8,128)(2,1)}, bf16[16,11,32,256]{3,2,1,0:T(8,128)(2,1)S(1)}, u32[]{:S(2)}, u32[]{:S(2)}) collective-permute-start(bf16[16,11,32,256]{3,2,1,0:T(8,128)(2,1)} %shard_map.355.refs_6_.refs_4_.refs_8_.refs_9_.refs_12_), channel_id=1, source_target_pairs={{0,1},{1,0},{2,3},{3,2},{4,5},{5,4},{6,7},{7,6},{8,9},{9,8},{10,11... | collective-permute-start | bytes 8650760 | tf_op jit(solution)/shard_map/ppermute | solution.py:803
  89.9 9.4 %collective-permute-start.19 = (bf16[3,2,1,8,512]{4,3,2,1,0:T(8,128)(2,1)S(1)}, bf16[3,2,1,8,512]{4,3,2,1,0:T(8,128)(2,1)S(1)}, u32[]{:S(2)}, u32[]{:S(2)}) collective-permute-start(bf16[3,2,1,8,512]{4,3,2,1,0:T(8,128)(2,1)S(1)} %get-tuple-element.245), channel_id=1, source_target_pairs={{0,1},{1,2},{2,3},{3,4},{4,5},{5,6},{6,7},{7,8},{8,9},{9,10},{10,1... | collective-permute-start | bytes 147464 | tf_op jit(solution)/shard_map/ppermute | solution.py:807
  92.3 7.1 %collective-permute-start.20 = (bf16[3,2,1,8,512]{4,3,2,1,0:T(8,128)(2,1)S(1)}, bf16[3,2,1,8,512]{4,3,2,1,0:T(8,128)(2,1)S(1)}, u32[]{:S(2)}, u32[]{:S(2)}) collective-permute-start(bf16[3,2,1,8,512]{4,3,2,1,0:T(8,128)(2,1)S(1)} %get-tuple-element.244), channel_id=1, source_target_pairs={{1,0},{2,1},{3,2},{4,3},{5,4},{6,5},{7,6},{8,7},{9,8},{10,9},{11,1... | collective-permute-start | bytes 147464 | tf_op jit(solution)/shard_map/ppermute | solution.py:807
  93.8 5.7 %collective-permute-start.10 = (f32[32,512]{1,0:T(8,128)S(1)}, f32[32,512]{1,0:T(8,128)S(1)}, u32[]{:S(2)}, u32[]{:S(2)}) collective-permute-start(f32[32,512]{1,0:T(8,128)S(1)} %get-tuple-element.76), channel_id=1, source_target_pairs={{1,0},{2,1},{3,2},{4,3},{5,4},{6,5},{7,6},{8,7},{9,8},{10,9},{11,1... | collective-permute-start | bytes 196616 | tf_op jit(solution)/shard_map/ppermute | solution.py:807
  112.1 5.4 collective-permute-start.24
  121.5 7.3 %collective-permute-start.27 = (f32[1,4,512]{2,1,0:T(4,128)S(1)}, f32[1,4,512]{2,1,0:T(4,128)S(1)}, u32[]{:S(2)}, u32[]{:S(2)}) collective-permute-start(f32[1,4,512]{2,1,0:T(4,128)S(1)} %pad_maximum_fusion.12), channel_id=1, source_target_pairs={{0,8},{1,9},{2,10},{3,11},{4,12},{5,13},{6,14},{7,15},{8,0},{9,1},... | collective-permute-start | bytes 24584 | tf_op jit(solution)/shard_map/ppermute | solution.py:803
  125.6 5.6 collective-permute-start.29
  126.1 5.3 collective-permute-start.21
  154.1 5.6 collective-permute-start.36
  177.0 11.5 %collective-permute-start.44 = (bf16[16,27,32,256]{3,2,1,0:T(8,128)(2,1)}, bf16[16,27,32,256]{3,2,1,0:T(8,128)(2,1)S(1)}, u32[]{:S(2)}, u32[]{:S(2)}) collective-permute-start(bf16[16,27,32,256]{3,2,1,0:T(8,128)(2,1)} %shard_map.359.refs_5_.refs_11_), channel_id=1, source_target_pairs={{0,1},{1,0},{2,3},{3,2},{4,5},{5,4},{6,7},{7,6},{8,9},{9,8},{10,11... | collective-permute-start | bytes 21233672 | tf_op jit(solution)/shard_map/ppermute | solution.py:803
  178.0 5.8 %collective-permute-start.43 = (f32[3,4,512]{2,1,0:T(4,128)}, f32[3,4,512]{2,1,0:T(4,128)S(1)}, u32[]{:S(2)}, u32[]{:S(2)}) collective-permute-start(f32[3,4,512]{2,1,0:T(4,128)} %pad_maximum_fusion.5.refs_1_), channel_id=1, source_target_pairs={{0,24},{1,25},{2,26},{3,27},{4,28},{5,29},{6,30},{7,31},{8,16},{9,... | collective-permute-start | bytes 73736 | tf_op jit(solution)/shard_map/ppermute | solution.py:803
  218.9 8.7 %collective-permute-start.51 = (f32[3,4,512]{2,1,0:T(4,128)S(1)}, f32[3,4,512]{2,1,0:T(4,128)S(1)}, u32[]{:S(2)}, u32[]{:S(2)}) collective-permute-start(f32[3,4,512]{2,1,0:T(4,128)S(1)} %pad_maximum_fusion.7), channel_id=1, source_target_pairs={{0,8},{1,9},{2,10},{3,11},{4,12},{5,13},{6,14},{7,15},{8,0},{9,1},... | collective-permute-start | bytes 73736 | tf_op jit(solution)/shard_map/ppermute | solution.py:803
  219.1 8.5 %collective-permute-start.52 = (f32[3,4,512]{2,1,0:T(4,128)S(1)}, f32[3,4,512]{2,1,0:T(4,128)S(1)}, u32[]{:S(2)}, u32[]{:S(2)}) collective-permute-start(f32[3,4,512]{2,1,0:T(4,128)S(1)} %pad_maximum_fusion.7), channel_id=1, source_target_pairs={{0,16},{1,17},{2,18},{3,19},{4,20},{5,21},{6,22},{7,23},{8,24},{9,... | collective-permute-start | bytes 73736 | tf_op jit(solution)/shard_map/ppermute | solution.py:803
  221.1 6.5 %collective-permute-start.53 = (f32[3,4,512]{2,1,0:T(4,128)S(1)}, f32[3,4,512]{2,1,0:T(4,128)S(1)}, u32[]{:S(2)}, u32[]{:S(2)}) collective-permute-start(f32[3,4,512]{2,1,0:T(4,128)S(1)} %pad_maximum_fusion.7), channel_id=1, source_target_pairs={{0,24},{1,25},{2,26},{3,27},{4,28},{5,29},{6,30},{7,31},{8,16},{9,... | collective-permute-start | bytes 73736 | tf_op jit(solution)/shard_map/ppermute | solution.py:803
  251.3 5.6 collective-permute-start.60
  289.8 30.4 %collective-permute-start.72 = (bf16[16,9,32,256]{3,2,1,0:T(8,128)(2,1)S(1)}, bf16[16,9,32,256]{3,2,1,0:T(8,128)(2,1)S(1)}, u32[]{:S(2)}, u32[]{:S(2)}) collective-permute-start(bf16[16,9,32,256]{3,2,1,0:T(8,128)(2,1)S(1)} %get-tuple-element.101), channel_id=1, source_target_pairs={{0,1},{1,0},{2,3},{3,2},{4,5},{5,4},{6,7},{7,6},{8,9},{9,8},{10,11... | collective-permute-start | bytes 7077896 | tf_op jit(solution)/shard_map/ppermute | solution.py:803
  299.3 5.6 collective-permute-start.67
  324.6 16.8 %collective-permute-start.76 = (bf16[8,9,32,256]{3,2,1,0:T(8,128)(2,1)}, bf16[8,9,32,256]{3,2,1,0:T(8,128)(2,1)S(1)}, u32[]{:S(2)}, u32[]{:S(2)}) collective-permute-start(bf16[8,9,32,256]{3,2,1,0:T(8,128)(2,1)} %shard_map.365.refs_1_), channel_id=1, source_target_pairs={{0,2},{1,5},{2,0},{3,7},{4,6},{5,1},{6,4},{7,3},{8,10},{9,13},{10,... | collective-permute-start | bytes 3538952 | tf_op jit(solution)/shard_map/ppermute | solution.py:803
  327.8 5.7 %collective-permute-start.75 = (f32[1,4,512]{2,1,0:T(4,128)}, f32[1,4,512]{2,1,0:T(4,128)S(1)}, u32[]{:S(2)}, u32[]{:S(2)}) collective-permute-start(f32[1,4,512]{2,1,0:T(4,128)} %shard_map.366), channel_id=1, source_target_pairs={{0,24},{1,25},{2,26},{3,27},{4,28},{5,29},{6,30},{7,31},{8,16},{9,... | collective-permute-start | bytes 24584 | tf_op jit(solution)/shard_map/ppermute | solution.py:803
  354.5 11.3 %collective-permute-start.83 = (bf16[16,9,32,256]{3,2,1,0:T(8,128)(2,1)}, bf16[16,9,32,256]{3,2,1,0:T(8,128)(2,1)S(1)}, u32[]{:S(2)}, u32[]{:S(2)}) collective-permute-start(bf16[16,9,32,256]{3,2,1,0:T(8,128)(2,1)} %shard_map.370), channel_id=1, source_target_pairs={{0,1},{1,0},{2,3},{3,2},{4,5},{5,4},{6,7},{7,6},{8,9},{9,8},{10,11... | collective-permute-start | bytes 7077896 | tf_op jit(solution)/shard_map/ppermute | solution.py:803
  355.6 10.2 %collective-permute-start.84 = (bf16[4,9,32,256]{3,2,1,0:T(8,128)(2,1)S(1)}, bf16[4,9,32,256]{3,2,1,0:T(8,128)(2,1)S(1)}, u32[]{:S(2)}, u32[]{:S(2)}) collective-permute-start(bf16[4,9,32,256]{3,2,1,0:T(8,128)(2,1)S(1)} %copy-done.39), channel_id=1, source_target_pairs={{0,4},{1,3},{2,6},{3,1},{4,0},{5,7},{6,2},{7,5},{8,12},{9,11},{10,... | collective-permute-start | bytes 1769480 | tf_op jit(solution)/shard_map/ppermute | solution.py:803
  358.2 7.5 %collective-permute-start.81 = (f32[1,4,512]{2,1,0:T(4,128)S(1)}, f32[1,4,512]{2,1,0:T(4,128)S(1)}, u32[]{:S(2)}, u32[]{:S(2)}) collective-permute-start(f32[1,4,512]{2,1,0:T(4,128)S(1)} %copy-done.135), channel_id=1, source_target_pairs={{0,4},{1,5},{2,6},{3,7},{4,0},{5,1},{6,2},{7,3},{8,12},{9,13},{10,... | collective-permute-start | bytes 24584 | tf_op jit(solution)/shard_map/ppermute | solution.py:803
  359.5 6.2 %collective-permute-start.82 = (f32[1,4,512]{2,1,0:T(4,128)S(1)}, f32[1,4,512]{2,1,0:T(4,128)S(1)}, u32[]{:S(2)}, u32[]{:S(2)}) collective-permute-start(f32[1,4,512]{2,1,0:T(4,128)S(1)} %copy-done.135), channel_id=1, source_target_pairs={{0,6},{1,7},{2,4},{3,5},{4,2},{5,3},{6,0},{7,1},{8,14},{9,15},{10,... | collective-permute-start | bytes 24584 | tf_op jit(solution)/shard_map/ppermute | solution.py:803
  370.2 17.5 %collective-permute-start.88 = (bf16[8,9,32,256]{3,2,1,0:T(8,128)(2,1)}, bf16[8,9,32,256]{3,2,1,0:T(8,128)(2,1)}, u32[]{:S(2)}, u32[]{:S(2)}) collective-permute-start(bf16[8,9,32,256]{3,2,1,0:T(8,128)(2,1)} %shard_map.371.refs_1_), channel_id=1, source_target_pairs={{0,2},{1,5},{2,0},{3,7},{4,6},{5,1},{6,4},{7,3},{8,10},{9,13},{10,... | collective-permute-start | bytes 3538952 | tf_op jit(solution)/shard_map/ppermute | solution.py:803
  372.2 5.7 %collective-permute-start.85 = (f32[1,4,512]{2,1,0:T(4,128)}, f32[1,4,512]{2,1,0:T(4,128)S(1)}, u32[]{:S(2)}, u32[]{:S(2)}) collective-permute-start(f32[1,4,512]{2,1,0:T(4,128)} %shard_map.372), channel_id=1, source_target_pairs={{0,8},{1,9},{2,10},{3,11},{4,12},{5,13},{6,14},{7,15},{8,0},{9,1},... | collective-permute-start | bytes 24584 | tf_op jit(solution)/shard_map/ppermute | solution.py:803
  372.2 7.0 %collective-permute-start.86 = (f32[1,4,512]{2,1,0:T(4,128)}, f32[1,4,512]{2,1,0:T(4,128)S(1)}, u32[]{:S(2)}, u32[]{:S(2)}) collective-permute-start(f32[1,4,512]{2,1,0:T(4,128)} %shard_map.372), channel_id=1, source_target_pairs={{0,16},{1,17},{2,18},{3,19},{4,20},{5,21},{6,22},{7,23},{8,24},{9,... | collective-permute-start | bytes 24584 | tf_op jit(solution)/shard_map/ppermute | solution.py:803
  374.1 5.7 %collective-permute-start.87 = (f32[1,4,512]{2,1,0:T(4,128)}, f32[1,4,512]{2,1,0:T(4,128)S(1)}, u32[]{:S(2)}, u32[]{:S(2)}) collective-permute-start(f32[1,4,512]{2,1,0:T(4,128)} %shard_map.372), channel_id=1, source_target_pairs={{0,24},{1,25},{2,26},{3,27},{4,28},{5,29},{6,30},{7,31},{8,16},{9,... | collective-permute-start | bytes 24584 | tf_op jit(solution)/shard_map/ppermute | solution.py:803
  376.6 9.8 %collective-permute-start.77 = (f32[32,512]{1,0:T(8,128)}, f32[32,512]{1,0:T(8,128)S(1)}, u32[]{:S(2)}, u32[]{:S(2)}) collective-permute-start(f32[32,512]{1,0:T(8,128)} %get-tuple-element.105), channel_id=1, source_target_pairs={{0,1},{1,2},{2,3},{3,4},{4,5},{5,6},{6,7},{7,8},{8,9},{9,10},{10,1... | collective-permute-start | bytes 196616 | tf_op jit(solution)/shard_map/ppermute | solution.py:807
  377.9 8.5 %collective-permute-start.78 = (f32[32,512]{1,0:T(8,128)S(1)}, f32[32,512]{1,0:T(8,128)S(1)}, u32[]{:S(2)}, u32[]{:S(2)}) collective-permute-start(f32[32,512]{1,0:T(8,128)S(1)} %get-tuple-element.106), channel_id=1, source_target_pairs={{1,0},{2,1},{3,2},{4,3},{5,4},{6,5},{7,6},{8,7},{9,8},{10,9},{11,1... | collective-permute-start | bytes 196616 | tf_op jit(solution)/shard_map/ppermute | solution.py:807
  402.5 12.6 %collective-permute-start.95 = (bf16[16,9,32,256]{3,2,1,0:T(8,128)(2,1)}, bf16[16,9,32,256]{3,2,1,0:T(8,128)(2,1)S(1)}, u32[]{:S(2)}, u32[]{:S(2)}) collective-permute-start(bf16[16,9,32,256]{3,2,1,0:T(8,128)(2,1)} %shard_map.376), channel_id=1, source_target_pairs={{0,1},{1,0},{2,3},{3,2},{4,5},{5,4},{6,7},{7,6},{8,9},{9,8},{10,11... | collective-permute-start | bytes 7077896 | tf_op jit(solution)/shard_map/ppermute | solution.py:803
  403.5 11.5 %collective-permute-start.96 = (bf16[4,9,32,256]{3,2,1,0:T(8,128)(2,1)S(1)}, bf16[4,9,32,256]{3,2,1,0:T(8,128)(2,1)S(1)}, u32[]{:S(2)}, u32[]{:S(2)}) collective-permute-start(bf16[4,9,32,256]{3,2,1,0:T(8,128)(2,1)S(1)} %copy-done.37), channel_id=1, source_target_pairs={{0,4},{1,3},{2,6},{3,1},{4,0},{5,7},{6,2},{7,5},{8,12},{9,11},{10,... | collective-permute-start | bytes 1769480 | tf_op jit(solution)/shard_map/ppermute | solution.py:803
  406.9 8.1 %collective-permute-start.93 = (f32[1,4,512]{2,1,0:T(4,128)S(1)}, f32[1,4,512]{2,1,0:T(4,128)S(1)}, u32[]{:S(2)}, u32[]{:S(2)}) collective-permute-start(f32[1,4,512]{2,1,0:T(4,128)S(1)} %copy-done.136), channel_id=1, source_target_pairs={{0,4},{1,5},{2,6},{3,7},{4,0},{5,1},{6,2},{7,3},{8,12},{9,13},{10,... | collective-permute-start | bytes 24584 | tf_op jit(solution)/shard_map/ppermute | solution.py:803
  407.5 7.5 %collective-permute-start.94 = (f32[1,4,512]{2,1,0:T(4,128)S(1)}, f32[1,4,512]{2,1,0:T(4,128)S(1)}, u32[]{:S(2)}, u32[]{:S(2)}) collective-permute-start(f32[1,4,512]{2,1,0:T(4,128)S(1)} %copy-done.136), channel_id=1, source_target_pairs={{0,6},{1,7},{2,4},{3,5},{4,2},{5,3},{6,0},{7,1},{8,14},{9,15},{10,... | collective-permute-start | bytes 24584 | tf_op jit(solution)/shard_map/ppermute | solution.py:803
  419.4 26.1 %collective-permute-start.100 = (bf16[8,9,32,256]{3,2,1,0:T(8,128)(2,1)}, bf16[8,9,32,256]{3,2,1,0:T(8,128)(2,1)}, u32[]{:S(2)}, u32[]{:S(2)}) collective-permute-start(bf16[8,9,32,256]{3,2,1,0:T(8,128)(2,1)} %shard_map.377.refs_1_), channel_id=1, source_target_pairs={{0,2},{1,5},{2,0},{3,7},{4,6},{5,1},{6,4},{7,3},{8,10},{9,13},{10,... | collective-permute-start | bytes 3538952 | tf_op jit(solution)/shard_map/ppermute | solution.py:803
  420.0 5.9 %collective-permute-start.97 = (f32[1,4,512]{2,1,0:T(4,128)}, f32[1,4,512]{2,1,0:T(4,128)S(1)}, u32[]{:S(2)}, u32[]{:S(2)}) collective-permute-start(f32[1,4,512]{2,1,0:T(4,128)} %shard_map.378), channel_id=1, source_target_pairs={{0,8},{1,9},{2,10},{3,11},{4,12},{5,13},{6,14},{7,15},{8,0},{9,1},... | collective-permute-start | bytes 24584 | tf_op jit(solution)/shard_map/ppermute | solution.py:803
  421.0 6.5 %collective-permute-start.98 = (f32[1,4,512]{2,1,0:T(4,128)}, f32[1,4,512]{2,1,0:T(4,128)S(1)}, u32[]{:S(2)}, u32[]{:S(2)}) collective-permute-start(f32[1,4,512]{2,1,0:T(4,128)} %shard_map.378), channel_id=1, source_target_pairs={{0,16},{1,17},{2,18},{3,19},{4,20},{5,21},{6,22},{7,23},{8,24},{9,... | collective-permute-start | bytes 24584 | tf_op jit(solution)/shard_map/ppermute | solution.py:803
  423.7 5.7 %collective-permute-start.99 = (f32[1,4,512]{2,1,0:T(4,128)}, f32[1,4,512]{2,1,0:T(4,128)S(1)}, u32[]{:S(2)}, u32[]{:S(2)}) collective-permute-start(f32[1,4,512]{2,1,0:T(4,128)} %shard_map.378), channel_id=1, source_target_pairs={{0,24},{1,25},{2,26},{3,27},{4,28},{5,29},{6,30},{7,31},{8,16},{9,... | collective-permute-start | bytes 24584 | tf_op jit(solution)/shard_map/ppermute | solution.py:803
  424.4 21.0 %collective-permute-start.89 = (f32[32,512]{1,0:T(8,128)}, f32[32,512]{1,0:T(8,128)S(1)}, u32[]{:S(2)}, u32[]{:S(2)}) collective-permute-start(f32[32,512]{1,0:T(8,128)} %get-tuple-element.111), channel_id=1, source_target_pairs={{0,1},{1,2},{2,3},{3,4},{4,5},{5,6},{6,7},{7,8},{8,9},{9,10},{10,1... | collective-permute-start | bytes 196616 | tf_op jit(solution)/shard_map/ppermute | solution.py:807
  425.9 19.5 %collective-permute-start.90 = (f32[32,512]{1,0:T(8,128)}, f32[32,512]{1,0:T(8,128)S(1)}, u32[]{:S(2)}, u32[]{:S(2)}) collective-permute-start(f32[32,512]{1,0:T(8,128)} %get-tuple-element.112), channel_id=1, source_target_pairs={{1,0},{2,1},{3,2},{4,3},{5,4},{6,5},{7,6},{8,7},{9,8},{10,9},{11,1... | collective-permute-start | bytes 196616 | tf_op jit(solution)/shard_map/ppermute | solution.py:807
  449.4 18.9 %collective-permute-start.103 = (bf16[16,11,32,256]{3,2,1,0:T(8,128)(2,1)}, bf16[16,11,32,256]{3,2,1,0:T(8,128)(2,1)}, u32[]{:S(2)}, u32[]{:S(2)}) collective-permute-start(bf16[16,11,32,256]{3,2,1,0:T(8,128)(2,1)} %shard_map.384), channel_id=1, source_target_pairs={{0,1},{1,0},{2,3},{3,2},{4,5},{5,4},{6,7},{7,6},{8,9},{9,8},{10,11... | collective-permute-start | bytes 8650760 | tf_op jit(solution)/shard_map/ppermute | solution.py:803
  450.4 11.6 %collective-permute-start.101 = (bf16[4,9,32,256]{3,2,1,0:T(8,128)(2,1)S(1)}, bf16[4,9,32,256]{3,2,1,0:T(8,128)(2,1)S(1)}, u32[]{:S(2)}, u32[]{:S(2)}) collective-permute-start(bf16[4,9,32,256]{3,2,1,0:T(8,128)(2,1)S(1)} %copy-done.24), channel_id=1, source_target_pairs={{0,4},{1,3},{2,6},{3,1},{4,0},{5,7},{6,2},{7,5},{8,12},{9,11},{10,... | collective-permute-start | bytes 1769480 | tf_op jit(solution)/shard_map/ppermute | solution.py:803
  471.7 21.6 %collective-permute-start.105 = (bf16[8,11,32,256]{3,2,1,0:T(8,128)(2,1)S(1)}, bf16[8,11,32,256]{3,2,1,0:T(8,128)(2,1)S(1)}, u32[]{:S(2)}, u32[]{:S(2)}) collective-permute-start(bf16[8,11,32,256]{3,2,1,0:T(8,128)(2,1)S(1)} %shard_map.385.refs_2_), channel_id=1, source_target_pairs={{0,2},{1,5},{2,0},{3,7},{4,6},{5,1},{6,4},{7,3},{8,10},{9,13},{10,... | collective-permute-start | bytes 4325384 | tf_op jit(solution)/shard_map/ppermute | solution.py:803
  477.5 31.7 %collective-permute-start.104 = (bf16[8,9,32,256]{3,2,1,0:T(8,128)(2,1)}, bf16[8,9,32,256]{3,2,1,0:T(8,128)(2,1)}, u32[]{:S(2)}, u32[]{:S(2)}) collective-permute-start(bf16[8,9,32,256]{3,2,1,0:T(8,128)(2,1)} %shard_map.386.refs_7_), channel_id=1, source_target_pairs={{0,2},{1,5},{2,0},{3,7},{4,6},{5,1},{6,4},{7,3},{8,10},{9,13},{10,... | collective-permute-start | bytes 3538952 | tf_op jit(solution)/shard_map/ppermute | solution.py:803
  481.1 33.2 %collective-permute-start.112 = (bf16[27,32,256]{2,1,0:T(8,128)(2,1)}, bf16[27,32,256]{2,1,0:T(8,128)(2,1)}, u32[]{:S(2)}, u32[]{:S(2)}) collective-permute-start(bf16[27,32,256]{2,1,0:T(8,128)(2,1)} %copy-done.45), channel_id=1, source_target_pairs={{0,16},{1,17},{2,18},{3,19},{4,20},{5,21},{6,22},{7,23},{8,24},{9,... | collective-permute-start | bytes 1327112 | tf_op jit(solution)/shard_map/ppermute | solution.py:803
  481.9 32.5 %collective-permute-start.113 = (bf16[27,32,256]{2,1,0:T(8,128)(2,1)}, bf16[27,32,256]{2,1,0:T(8,128)(2,1)}, u32[]{:S(2)}, u32[]{:S(2)}) collective-permute-start(bf16[27,32,256]{2,1,0:T(8,128)(2,1)} %copy-done.71), channel_id=1, source_target_pairs={{0,8},{1,9},{2,10},{3,11},{4,12},{5,13},{6,14},{7,15},{8,0},{9,1},... | collective-permute-start | bytes 1327112 | tf_op jit(solution)/shard_map/ppermute | solution.py:803
  484.6 29.8 %collective-permute-start.114 = (bf16[27,32,256]{2,1,0:T(8,128)(2,1)}, bf16[27,32,256]{2,1,0:T(8,128)(2,1)}, u32[]{:S(2)}, u32[]{:S(2)}) collective-permute-start(bf16[27,32,256]{2,1,0:T(8,128)(2,1)} %copy-done.70), channel_id=1, source_target_pairs={{0,24},{1,25},{2,26},{3,27},{4,28},{5,29},{6,30},{7,31},{8,16},{9,... | collective-permute-start | bytes 1327112 | tf_op jit(solution)/shard_map/ppermute | solution.py:803
  496.1 25.7 %collective-permute-start.107 = (bf16[4,11,32,256]{3,2,1,0:T(8,128)(2,1)S(1)}, bf16[4,11,32,256]{3,2,1,0:T(8,128)(2,1)}, u32[]{:S(2)}, u32[]{:S(2)}) collective-permute-start(bf16[4,11,32,256]{3,2,1,0:T(8,128)(2,1)S(1)} %shard_map.388.refs_3_), channel_id=1, source_target_pairs={{0,4},{1,3},{2,6},{3,1},{4,0},{5,7},{6,2},{7,5},{8,12},{9,11},{10,... | collective-permute-start | bytes 2162696 | tf_op jit(solution)/shard_map/ppermute | solution.py:803
  511.6 10.2 %collective-permute-start.106 = (bf16[4,9,32,256]{3,2,1,0:T(8,128)(2,1)}, bf16[4,9,32,256]{3,2,1,0:T(8,128)(2,1)}, u32[]{:S(2)}, u32[]{:S(2)}) collective-permute-start(bf16[4,9,32,256]{3,2,1,0:T(8,128)(2,1)} %shard_map.389), channel_id=1, source_target_pairs={{0,4},{1,3},{2,6},{3,1},{4,0},{5,7},{6,2},{7,5},{8,12},{9,11},{10,... | collective-permute-start | bytes 1769480 | tf_op jit(solution)/shard_map/ppermute | solution.py:803
  515.9 37.6 %collective-permute-start.115 = (f32[27,32,256]{2,1,0:T(8,128)S(1)}, f32[27,32,256]{2,1,0:T(8,128)S(1)}, u32[]{:S(2)}, u32[]{:S(2)}) collective-permute-start(f32[27,32,256]{2,1,0:T(8,128)S(1)} %convert_add_fusion), channel_id=1, source_target_pairs={{0,1},{1,0},{2,3},{3,2},{4,5},{5,4},{6,7},{7,6},{8,9},{9,8},{10,11... | collective-permute-start | bytes 2654216 | tf_op jit(solution)/shard_map/ppermute | solution.py:803
  524.7 19.6 %collective-permute-start.108 = (bf16[20,32,256]{2,1,0:T(8,128)(2,1)S(1)}, bf16[20,32,256]{2,1,0:T(8,128)(2,1)S(1)}, u32[]{:S(2)}, u32[]{:S(2)}) collective-permute-start(bf16[20,32,256]{2,1,0:T(8,128)(2,1)S(1)} %get-tuple-element.129), channel_id=1, source_target_pairs={{0,16},{1,17},{2,18},{3,19},{4,20},{5,21},{6,22},{7,23},{8,24},{9,... | collective-permute-start | bytes 983048 | tf_op jit(solution)/shard_map/ppermute | solution.py:803
  528.7 15.9 %collective-permute-start.109 = (bf16[20,32,256]{2,1,0:T(8,128)(2,1)S(1)}, bf16[20,32,256]{2,1,0:T(8,128)(2,1)S(1)}, u32[]{:S(2)}, u32[]{:S(2)}) collective-permute-start(bf16[20,32,256]{2,1,0:T(8,128)(2,1)S(1)} %get-tuple-element.130), channel_id=1, source_target_pairs={{0,8},{1,9},{2,10},{3,11},{4,12},{5,13},{6,14},{7,15},{8,0},{9,1},... | collective-permute-start | bytes 983048 | tf_op jit(solution)/shard_map/ppermute | solution.py:803
  528.7 23.3 %collective-permute-start.110 = (bf16[20,32,256]{2,1,0:T(8,128)(2,1)S(1)}, bf16[20,32,256]{2,1,0:T(8,128)(2,1)S(1)}, u32[]{:S(2)}, u32[]{:S(2)}) collective-permute-start(bf16[20,32,256]{2,1,0:T(8,128)(2,1)S(1)} %get-tuple-element.131), channel_id=1, source_target_pairs={{0,24},{1,25},{2,26},{3,27},{4,28},{5,29},{6,30},{7,31},{8,16},{9,... | collective-permute-start | bytes 983048 | tf_op jit(solution)/shard_map/ppermute | solution.py:803
  (246 other events, 3315.6 us)
Sparse Core Ops, SparseCore 0:
  11.4 72.8 all-gather.4
  86.4 82.7 all-gather.6
